TPU v7x, 512 devices: a whole 4x4x16 slice. The times are simulated.
512 devices in a mesh: seq: 64 (over x, z), head: 8 (over y, core).
Axes of the slice: x: 4, y: 4, z: 16, core: 2. Of those that a mesh axis runs over, the one named last changes fastest.
Arguments:
- lat_query: bfloat16 [256, 1024], P(None, 'head'), may hold values from -20 to 20
- pkt_key: bfloat16 [147456, 1024], P('seq', 'head'), may hold values from -20 to 20
- pkt_value: bfloat16 [147456, 1024], P('seq', 'head'), may hold values from -6 to 6
- enc_grad: bfloat16 [256, 1024], P(None, 'head'), may hold values from -6 to 6
- pkt_query: bfloat16 [147456, 1024], P('seq', 'head'), may hold values from -20 to 20
- lat_key: bfloat16 [256, 1024], P(None, 'head'), may hold values from -20 to 20
- lat_value: bfloat16 [256, 1024], P(None, 'head'), may hold values from -6 to 6
- dec_grad: bfloat16 [147456, 1024], P('seq', 'head'), may hold values from -6 to 6
- row_mask: int32 [147456], P(('seq', 'head')), may hold values 0 or 1
Outputs:
- grad_lat_query: bfloat16 [256, 1024], P(None, 'head')
- grad_pkt_key: bfloat16 [147456, 1024], P('seq', 'head')
- grad_pkt_value: bfloat16 [147456, 1024], P('seq', 'head')
- grad_pkt_query: bfloat16 [147456, 1024], P('seq', 'head')
- grad_lat_key: bfloat16 [256, 1024], P(None, 'head')
- grad_lat_value: float32 [256, 1024], P(None, 'head')
All inputs are finite; a program needn't handle non-finite values. No bound on the sum of `row_mask` on one device may be relied on, other than what follows from the above.
Results may differ from a plain program's by a relative error of at most 0.023.
Values sent between devices are 32-bit elements; how exact they have to be, the bound alone decides.
A program may use at most 64 MiB of HBM per device.

v0:
```python
import math

import jax
import jax.numpy as jnp
from jax import lax
from jax.sharding import PartitionSpec as P

DH = 128


def joined(value, axis, join):
    pieces = jax.tree.map(lambda part: lax.all_gather(part, axis), value)
    head = jax.tree.map(lambda part: part[0], pieces)
    tail = jax.tree.map(lambda part: part[1:], pieces)
    subtotal, _ = lax.scan(lambda subtotal, share: (join(subtotal, share), None), head, tail)
    return subtotal


def split_heads(array):
    return array.reshape(array.shape[0], -1, DH)


def join_local(array):
    return array.reshape(array.shape[0], -1)


def merge_partials(first, second):
    top = jnp.maximum(first[0], second[0])
    left = jnp.exp(first[0] - top)
    right = jnp.exp(second[0] - top)
    return (
        top,
        first[1] * left + second[1] * right,
        first[2] * left[..., None] + second[2] * right[..., None],
    )


def on_device(
    lat_query, pkt_key, pkt_value, enc_grad, pkt_query, lat_key, lat_value, dec_grad, row_mask
):
    scale = 1.0 / math.sqrt(DH)
    valid = lax.all_gather(row_mask, "head", axis=0, tiled=True) > 0
    query = split_heads(lat_query)
    keys = split_heads(pkt_key)
    values = split_heads(pkt_value)
    grad_out = split_heads(enc_grad)
    scores = jnp.einsum("lhd,rhd->hlr", query, keys, preferred_element_type=jnp.float32) * scale
    scores = jnp.where(valid[None, None, :], scores, -1e30)
    local_top = jnp.max(scores, axis=2)
    expo = jnp.where(valid[None, None, :], jnp.exp(scores - local_top[..., None]), 0.0)
    local_total = jnp.sum(expo, axis=2)
    dprob = jnp.einsum("lhd,rhd->hlr", grad_out, values, preferred_element_type=jnp.float32)
    weighted = jnp.einsum(
        "hlr,rhd->hld", expo.astype(jnp.bfloat16), values, preferred_element_type=jnp.float32
    )
    top, total, output = joined((local_top, local_total, weighted), "seq", merge_partials)
    probs = (
        jnp.where(valid[None, None, :], jnp.exp(scores - top[..., None]), 0.0) / total[..., None]
    )
    delta = jnp.einsum("lhd,hld->hl", grad_out.astype(jnp.float32), output) / total
    dscore = (probs * (dprob - delta[..., None])).astype(jnp.bfloat16)
    query_part = jnp.einsum("hlr,rhd->lhd", dscore, keys, preferred_element_type=jnp.float32)
    grad_pkt_key = (
        jnp.einsum("hlr,lhd->rhd", dscore, query, preferred_element_type=jnp.float32) * scale
    ).astype(jnp.bfloat16)
    grad_pkt_value = jnp.einsum(
        "hlr,lhd->rhd", probs.astype(jnp.bfloat16), grad_out, preferred_element_type=jnp.float32
    ).astype(jnp.bfloat16)
    query_total = lax.psum(query_part, "seq")
    dec_query = split_heads(pkt_query)
    dec_keys = split_heads(lat_key)
    dec_values = split_heads(lat_value)
    masked = jnp.where(valid[:, None, None], split_heads(dec_grad), jnp.zeros((), jnp.bfloat16))
    dscores = (
        jnp.einsum("rhd,lhd->hrl", dec_query, dec_keys, preferred_element_type=jnp.float32) * scale
    )
    dexpo = jnp.exp(dscores - jnp.max(dscores, axis=2, keepdims=True))
    dprobs = dexpo / jnp.sum(dexpo, axis=2, keepdims=True)
    ddprob = jnp.einsum("rhd,lhd->hrl", masked, dec_values, preferred_element_type=jnp.float32)
    ddelta = jnp.sum(dprobs * ddprob, axis=2, keepdims=True)
    ddscore = (dprobs * (ddprob - ddelta)).astype(jnp.bfloat16)
    grad_pkt_query = (
        jnp.einsum("hrl,lhd->rhd", ddscore, dec_keys, preferred_element_type=jnp.float32) * scale
    ).astype(jnp.bfloat16)
    key_part = jnp.einsum("hrl,rhd->lhd", ddscore, dec_query, preferred_element_type=jnp.float32)
    value_part = jnp.einsum(
        "hrl,rhd->lhd", dprobs.astype(jnp.bfloat16), masked, preferred_element_type=jnp.float32
    )
    key_total, value_total = lax.psum((key_part, value_part), "seq")
    query_grad = (query_total * scale).astype(jnp.bfloat16)
    key_grad = (key_total * scale).astype(jnp.bfloat16)
    return (
        join_local(query_grad),
        join_local(grad_pkt_key),
        join_local(grad_pkt_value),
        join_local(grad_pkt_query),
        join_local(key_grad),
        join_local(value_total),
    )


def solution(mesh):
    placed = (
        P(None, "head"),
        P("seq", "head"),
        P("seq", "head"),
        P(None, "head"),
        P("seq", "head"),
        P(None, "head"),
        P(None, "head"),
        P("seq", "head"),
        P(("seq", "head")),
    )
    return jax.shard_map(
        on_device,
        mesh=mesh,
        in_specs=placed,
        out_specs=(
            P(None, "head"),
            P("seq", "head"),
            P("seq", "head"),
            P("seq", "head"),
            P(None, "head"),
            P(None, "head"),
        ),
        check_vma=False,
    )
```

profile of v0, /device:TPU:24, one launch (start us, length us, event | category | flops | bytes accessed | tf_op | source)
XLA Modules:
  0.0 567.5 jit_solution(1385143227791440516)
XLA Ops:
  7.2 1.3 dynamic-slice
  10.1 24.6 %all-reduce = s32[2304]{0:T(1024)S(1)} all-reduce(s32[2304]{0:T(1024)S(1)} %dynamic-update-slice), channel_id=1, replica_groups=mesh['seq'=64,'head'=8] {'head'}, use_global_device_ids=true, to_apply=%add | all-reduce | flops 2304 | bytes 18432
  34.8 1.7 fusion.32
  36.5 1.2 fusion.12
  38.3 85.3 %all-gather.4 = f32[64,1,256]{2,1,0:T(1,128)S(1)} all-gather(f32[1,1,256]{2,1,0:T(1,128)S(1)} %bitcast.92), channel_id=3, replica_groups=mesh['seq'=64,'head'=8] {'seq'}, dimensions={0}, use_global_device_ids=true | all-gather | bytes 66560 | tf_op jit(solution)/shard_map/all_gather | solution.py:12
  123.6 80.6 %all-gather.3 = f32[64,1,256]{2,1,0:T(1,128)S(1)} all-gather(f32[1,1,256]{2,1,0:T(1,128)S(1)} %bitcast.91), channel_id=2, replica_groups=mesh['seq'=64,'head'=8] {'seq'}, dimensions={0}, use_global_device_ids=true | all-gather | bytes 66560 | tf_op jit(solution)/shard_map/all_gather | solution.py:12
  205.3 2.0 multiply_reduce_fusion
  207.9 1.1 convolution_bitcast_fusion
  209.0 1.3 fusion.7
  210.3 1.7 fusion.20
  212.1 5.7 slice.39
  218.7 70.5 %while.14 = (s32[]{:T(128)}, f32[1,256]{1,0:T(1,128)S(1)}, f32[1,256]{1,0:T(1,128)S(1)}, f32[1,256,128]{2,1,0:T(8,128)S(1)}, f32[63,1,256]{2,1,0:T(1,128)S(1)}, ...) while((s32[]{:T(128)}, f32[1,256]{1,0:T(1,128)S(1)}, f32[1,256]{1,0:T(1,128)S(1)}, ...), condition=%wide.region_3.4_spmd, body=%wide.region_2.3_spmd.sunk | while | flops 99842 | bytes 403549 | solution.py:15
  218.7 1.1 fusion.54
  219.9 1.1 fusion.54
  221.0 1.1 fusion.54
  222.1 1.1 fusion.54
  223.2 1.1 fusion.54
  224.3 1.1 fusion.54
  225.5 1.1 fusion.54
  226.6 1.1 fusion.54
  227.7 1.1 fusion.54
  228.8 1.1 fusion.54
  229.9 1.1 fusion.54
  231.0 1.1 fusion.54
  232.2 1.1 fusion.54
  233.3 1.1 fusion.54
  234.4 1.1 fusion.54
  235.5 1.1 fusion.54
  236.6 1.1 fusion.54
  237.8 1.1 fusion.54
  238.9 1.1 fusion.54
  240.0 1.1 fusion.54
  241.1 1.1 fusion.54
  242.2 1.1 fusion.54
  243.3 1.1 fusion.54
  244.5 1.1 fusion.54
  245.6 1.1 fusion.54
  246.7 1.1 fusion.54
  247.8 1.1 fusion.54
  248.9 1.1 fusion.54
  250.1 1.1 fusion.54
  251.2 1.1 fusion.54
  252.3 1.1 fusion.54
  253.4 1.1 fusion.54
  254.5 1.1 fusion.54
  255.7 1.1 fusion.54
  256.8 1.1 fusion.54
  257.9 1.1 fusion.54
  259.0 1.1 fusion.54
  260.1 1.1 fusion.54
  261.2 1.1 fusion.54
  262.4 1.1 fusion.54
  273.5 1.1 fusion.54
  274.7 1.1 fusion.54
  275.8 1.1 fusion.54
  276.9 1.1 fusion.54
  278.0 1.1 fusion.54
  289.3 1.8 fusion.5
  292.2 1.1 convolution_bitcast_fusion.1
  293.3 2.6 fusion.6
  296.0 1.6 convolution_convert_fusion
  297.6 259.8 %all-reduce.4.cloned.1.call-done = (f32[256,1,128]{2,0,1:T(8,128)}, f32[256,1,128]{2,0,1:T(8,128)}, f32[256,128]{0,1:T(8,128)}) async-done(((f32[256,1,128]{2,0,1:T(8,128)}, f32[256,1,128]{2,0,1:T(8,128)}, f32[256,128]{0,1:T(8,128)}), (f32[256,1,128]{2,0,1:T(8,128)}, f32[256,1,128]{2,0,1:T(8,128)}, f32[256,128]{0,1:T(8,128)})) %all-reduce.4.cloned.1.call-update) | async-done | bytes 393232 | tf_op jit(solution)/shard_map/psum | solution.py:69
  557.4 1.7 copy.18
  559.0 1.6 fusion.25
  (124 shorter events, 26.3 us)
Async XLA Ops:
  7.2 197.0 %copy-start = (bf16[2304,128]{1,0:T(8,128)(2,1)S(1)}, bf16[2304,128]{1,0:T(8,128)(2,1)}, u32[]{:S(2)}) copy-start(bf16[2304,128]{1,0:T(8,128)(2,1)} %param.15) | copy-start | bytes 1769476
  7.2 204.9 %all-gather.7.cloned.1.call-start = ((), (), s32[]{:S(2)}) async-start(), calls=%async_computation | async-start | bytes 8519680 | tf_op jit(solution)/shard_map/all_gather | solution.py:12
  34.7 1.7 copy-start.9
  36.5 167.7 %copy-start.3 = (bf16[256,128]{1,0:T(8,128)(2,1)S(1)}, bf16[256,128]{1,0:T(8,128)(2,1)}, u32[]{:S(2)}) copy-start(bf16[256,128]{1,0:T(8,128)(2,1)} %param.16) | copy-start | bytes 196612
  37.7 519.6 %all-reduce.4.cloned.1.call-start = ((), (), s32[]{:S(2)}) async-start(), calls=%async_computation.1 | async-start | bytes 786432 | tf_op jit(solution)/shard_map/psum | solution.py:69
  123.6 85.4 %copy-start.5 = (f32[64,1,256]{2,1,0:T(1,128)}, f32[64,1,256]{2,1,0:T(1,128)S(1)}, u32[]{:S(2)}) copy-start(f32[64,1,256]{2,1,0:T(1,128)S(1)} %all-gather.4) | copy-start | bytes 196612
  204.2 4.8 copy-start.6
  204.2 1.1 copy-start.8
  204.2 1.1 copy-start.10
  212.1 6.6 %slice-start = ((f32[64,1,256]{2,1,0:T(1,128)}), f32[63,1,256]{2,1,0:T(1,128)S(1)}, s32[]{:S(2)}) async-start(f32[64,1,256]{2,1,0:T(1,128)} %copy-done.5), calls=%async_computation.2 | async-start | bytes 129024 | tf_op jit(solution)/shard_map/slice | solution.py:14
  212.1 6.6 %slice-start.1 = ((f32[64,1,256]{2,1,0:T(1,128)}), f32[63,1,256]{2,1,0:T(1,128)S(1)}, s32[]{:S(2)}) async-start(f32[64,1,256]{2,1,0:T(1,128)} %copy-done.6), calls=%async_computation.3 | async-start | bytes 129024 | tf_op jit(solution)/shard_map/slice | solution.py:14
  217.7 71.4 %copy-start.7 = (bf16[256,128]{1,0:T(8,128)(2,1)S(1)}, bf16[256,128]{1,0:T(8,128)(2,1)}, u32[]{:S(2)}) copy-start(bf16[256,128]{1,0:T(8,128)(2,1)} %param.14) | copy-start | bytes 196612
  289.3 2.9 copy-start.2
  289.3 4.0 copy-start.4
  291.2 1.0 copy-start.1
Sparse Core Ops, SparseCore 0:
  37.9 160.1 all-gather.6
  296.1 261.2 all-reduce.3
where the time goes:
time: 569 us; the launch traced here: 568 us
  waiting for transfers between devices  260 us (46%)
  blocking collectives  191 us (34%)
  other arithmetic  72.4 us (13%)
  matrix products  16.8 us (3%)
  between operations  14.9 us (3%)
  local copies, waits for them, and re-layouts  11.8 us (2%)
    psum x1, waiting for transfers between devices, on_device(): query_total = lax.psum(query_part, 'seq')  260 us
    all_gather x2, blocking collectives, joined(): pieces = jax.tree.map(lambda part: lax.all_gather(part, axis), value)  166 us
    add x63, other arithmetic, merge_partials(): first[2] * left[..., None] + second[2] * right[..., None]  67.5 us
    unnamed x1, blocking collectives  24.6 us
  transfers between devices with their start and end apart: 2, of which 1 were waited for; matrix products, arithmetic and copies ran while one was open for 2% of the time, Pallas kernels for 0%

commit v1 on v0

v1 whole, which is shorter than its diff:
```python
import functools
import math

import jax
import jax.numpy as jnp
from jax import lax
from jax.experimental import pallas as pl
from jax.experimental.pallas import tpu as pltpu
from jax.sharding import PartitionSpec as P

DH = 128
LAT = 256
NZ = 16
MESH = pl.DeviceIdType.MESH
F32 = jnp.float32
BF16 = jnp.bfloat16
NT = (((1,), (1,)), ((), ()))
NN = (((1,), (0,)), ((), ()))
TN = (((0,), (0,)), ((), ()))


def dot(a, b, dims):
    return lax.dot_general(a, b, dims, preferred_element_type=F32)


def merge_stats(ref, count):
    lses = [ref[i, 0:2, :] for i in range(count)]
    top = functools.reduce(jnp.maximum, lses)
    weights = [jnp.exp(lse - top) for lse in lses]
    total = functools.reduce(jnp.add, weights)
    mixed = functools.reduce(jnp.add, [w * ref[i, 2:4, :] for i, w in enumerate(weights)])
    return top + jnp.log(total), mixed / total


def fold(line):
    return jnp.concatenate([line[:, :128], line[:, 128:]], axis=0)


def kernel(
    nx, nh, rows,
    lq_hbm, pk_hbm, pv_hbm, eg_hbm, pq_hbm, lk_hbm, lv_hbm, dg_hbm, mask_hbm,
    glq_ref, gpk_ref, gpv_ref, gpq_ref, glk_ref, glv_ref,
    lq_ref, pk_ref, pv_ref, eg_ref, pq_ref, lk_ref, lv_ref, dg_ref, mask_ref,
    maskbuf, mcol, expo, edot, chunk_top, dprob, query_t,
    sx, sz, pdec, rxdec, sumdec, rzdec, fulldec, pq, rxq, sumq, rzq, fullq,
    in_sems,
    m_send, m_recv, sx_send, sx_recv, sz_send, sz_recv,
    dx_send, dx_recv, dz_send, dz_recv, daz_send, daz_recv, dax_send, dax_recv,
    qx_send, qx_recv, qz_send, qz_recv, qaz_send, qaz_recv, qax_send, qax_recv,
):
    scale = 1.0 / math.sqrt(DH)
    piece = rows // nh
    chunks = 4
    size = rows // chunks
    seq = lax.axis_index("seq")
    head = lax.axis_index("head")
    xi = seq // NZ
    zi = lax.rem(seq, NZ)

    loads = [
        pltpu.make_async_copy(src, dst, in_sems.at[i])
        for i, (src, dst) in enumerate(
            (
                (mask_hbm, mask_ref),
                (pq_hbm, pq_ref),
                (lk_hbm, lk_ref),
                (dg_hbm, dg_ref),
                (lv_hbm, lv_ref),
                (pk_hbm, pk_ref),
                (lq_hbm, lq_ref),
                (pv_hbm, pv_ref),
                (eg_hbm, eg_ref),
            )
        )
    ]
    for load in loads:
        load.start()

    def head_peer(step):
        return lax.rem(head + step, nh)

    def x_peer(step):
        return lax.rem(xi + step, nx)

    def z_peer(step):
        return lax.rem(zi + NZ // 2 + (step // 2) * (2 * lax.rem(step, 2) - 1), NZ)

    def at_head(peer):
        return (seq, peer)

    def at_x(peer):
        return (peer * NZ + zi, head)

    def at_z(peer):
        return (xi * NZ + peer, head)

    def every(count, body):
        def step(i, carry):
            body(i)
            return carry

        lax.fori_loop(1, count, step, 0)

    def send(src, dst, send_sem, recv_sem, target):
        return pltpu.make_async_remote_copy(
            src_ref=src, dst_ref=dst, send_sem=send_sem.at[0], recv_sem=recv_sem.at[0],
            device_id=target, device_id_type=MESH,
        )

    def all_of(ref, count, send_sem, recv_sem, target):
        part = ref.at[pl.ds(0, count - 1)]
        return send(part, part, send_sem, recv_sem, target)

    barrier = pltpu.get_barrier_semaphore()

    def greet(peer_of, place):
        def body(step):
            pl.semaphore_signal(
                barrier, inc=1, device_id=place(peer_of(step)), device_id_type=MESH
            )
        return body

    every(nh, greet(head_peer, at_head))
    every(nx, greet(x_peer, at_x))
    every(NZ, greet(z_peer, at_z))
    loads[0].wait()
    maskbuf[head] = jnp.zeros((1, 384), F32)
    maskbuf[head, :, 0:piece] = (mask_ref[...] > 0).astype(F32).reshape(1, piece)
    pl.semaphore_wait(barrier, nh + nx + NZ - 3)

    every(nh, lambda i: send(
        maskbuf.at[head], maskbuf.at[head], m_send, m_recv, at_head(head_peer(i))
    ).start())

    loads[1].wait()
    loads[2].wait()
    lat_key = lk_ref[...]

    def dec_probs(i, carry):
        span = pl.ds(pl.multiple_of(i * size, size), size)
        score = dot(pq_ref[span, :], lat_key, NT) * scale
        e = jnp.exp(score - jnp.max(score, axis=1, keepdims=True))
        dprob[span, :] = e * (1.0 / jnp.sum(e, axis=1, keepdims=True))
        return carry

    lax.fori_loop(0, chunks, dec_probs, 0)

    mask_all = all_of(maskbuf, nh, m_send, m_recv, at_head(head_peer(1)))
    mask_all.wait_recv()
    for h in range(nh):
        line = jnp.broadcast_to(maskbuf[h], (128, 384))
        mcol[h * piece:(h + 1) * piece, :] = line.T[:piece, :]

    loads[3].wait()
    loads[4].wait()
    lat_value = lv_ref[...]

    def dec_grads(i, carry):
        span = pl.ds(pl.multiple_of(i * size, size), size)
        masked = dg_ref[span, :] * mcol[span, :].astype(BF16)
        dg = dot(masked, lat_value, NT)
        p = dprob[span, :]
        dd = jnp.sum(p * dg, axis=1, keepdims=True)
        ds = (p * (dg - dd)).astype(BF16)
        gpq_ref[span, :] = (dot(ds, lat_key, NN) * scale).astype(BF16)
        key_t, value_t = carry
        key_t = key_t + dot(pq_ref[span, :], ds, TN)
        value_t = value_t + dot(masked, p.astype(BF16), TN)
        return key_t, value_t

    blank = jnp.zeros((DH, LAT), F32)
    key_t, value_t = lax.fori_loop(0, chunks, dec_grads, (blank, blank))
    pdec[0:nx // 2] = key_t.T.reshape(nx // 2, NZ, 8, 128)
    pdec[nx // 2:nx] = value_t.T.reshape(nx // 2, NZ, 8, 128)

    class Sum:
        def __init__(self, part, rx, summed, rz, full, *sems):
            self.part, self.rx, self.summed, self.rz, self.full = part, rx, summed, rz, full
            self.x_sems, self.z_sems = sems[0:2], sems[2:4]
            self.az_sems, self.ax_sems = sems[4:6], sems[6:8]
            self.whole = [
                all_of(rx, nx, *self.x_sems, at_x(x_peer(1))),
                all_of(rz, NZ, *self.z_sems, at_z(z_peer(1))),
                all_of(full.at[xi], NZ, *self.az_sems, at_z(z_peer(1))),
                all_of(full, nx, *self.ax_sems, at_x(x_peer(1))),
            ]

        def scatter_x(self):
            every(nx, lambda i: send(
                self.part.at[x_peer(i)], self.rx.at[xi], *self.x_sems, at_x(x_peer(i))
            ).start())

        def gathered_x(self):
            self.rx[xi] = self.part[xi]
            self.whole[0].wait_recv()

        def scatter_z(self):
            every(NZ, lambda i: send(
                self.summed.at[z_peer(i)], self.rz.at[zi], *self.z_sems, at_z(z_peer(i))
            ).start())

        def gather_z(self):
            self.rz[zi] = self.summed[zi]
            self.whole[1].wait_recv()
            pieces = [self.rz[i] for i in range(NZ)]
            while len(pieces) > 1:
                pieces = [a + b for a, b in zip(pieces[0::2], pieces[1::2])]
            self.full[xi, zi] = pieces[0]
            every(NZ, lambda i: send(
                self.full.at[xi, zi], self.full.at[xi, zi], *self.az_sems, at_z(z_peer(i))
            ).start())

        def gather_x(self):
            self.whole[2].wait_recv()
            every(nx, lambda i: send(
                self.full.at[xi], self.full.at[xi], *self.ax_sems, at_x(x_peer(i))
            ).start())

        def finish(self):
            self.whole[3].wait_recv()

        def drain(self):
            for copy in self.whole:
                copy.wait_send()

    dec = Sum(
        pdec, rxdec, sumdec, rzdec, fulldec,
        dx_send, dx_recv, dz_send, dz_recv, daz_send, daz_recv, dax_send, dax_recv,
    )
    enc = Sum(
        pq, rxq, sumq, rzq, fullq,
        qx_send, qx_recv, qz_send, qz_recv, qaz_send, qaz_recv, qax_send, qax_recv,
    )
    dec.scatter_x()

    for load in loads[5:]:
        load.wait()
    lat_query = lq_ref[...]
    enc_grad = eg_ref[...]

    def enc_first(i, carry):
        top, total, delta, a, b = carry
        span = pl.ds(pl.multiple_of(i * size, size), size)
        keys = pk_ref[span, :]
        bias = (mcol[span, :] - 1.0) * 1e30
        score = dot(keys, lat_query, NT) * scale
        score = score + jnp.concatenate([bias, bias], axis=1)
        grad = dot(pv_ref[span, :], enc_grad, NT)
        own = jnp.max(score, axis=0, keepdims=True)
        e = jnp.exp(score - own)
        expo[span, :] = e
        edot[span, :] = grad
        chunk_top[i] = own
        own_total = jnp.sum(e, axis=0, keepdims=True)
        own_delta = jnp.sum(e * grad, axis=0, keepdims=True) / own_total
        ds = (e * (grad - own_delta)).astype(BF16)
        sums = dot(keys, jnp.concatenate([ds, e.astype(BF16)], axis=1), TN)
        own_a, own_b = sums[:, :LAT], sums[:, LAT:]
        later = jnp.maximum(top, own)
        left = jnp.exp(top - later)
        right = jnp.exp(own - later)
        both = total * left + own_total * right
        mixed = (total * left * delta + own_total * right * own_delta) / both
        a = left * (a + (delta - mixed) * b) + right * (own_a + (own_delta - mixed) * own_b)
        b = left * b + right * own_b
        return later, both, mixed, a, b

    zero = jnp.zeros((1, LAT), F32)
    top, total, delta, a, b = lax.fori_loop(
        0, chunks, enc_first, (jnp.full((1, LAT), -3e30, F32), zero, zero, blank, blank)
    )

    def put_stats(ref, slot, lse_rows, delta_rows):
        ref[slot, 0:2, :] = lse_rows
        ref[slot, 2:4, :] = delta_rows

    put_stats(sx, xi, fold(top + jnp.log(total)), fold(delta))
    every(nx, lambda i: send(sx.at[xi], sx.at[xi], sx_send, sx_recv, at_x(x_peer(i))).start())

    share = 1.0 / total
    a = a * share
    b = b * share

    def place(i, j):
        at = i * (DH // nx) + (j // 2) * 4
        return slice(at, at + 4), slice((j % 2) * 128, (j % 2) * 128 + 128)

    for i in range(nx):
        for j in range(NZ):
            pq[i, j] = jnp.concatenate([a[place(i, j)], b[place(i, j)]], axis=0)
    enc.scatter_x()

    sx_all = all_of(sx, nx, sx_send, sx_recv, at_x(x_peer(1)))
    sx_all.wait_recv()
    put_stats(sz, zi, *merge_stats(sx, nx))
    every(NZ, lambda i: send(sz.at[zi], sz.at[zi], sz_send, sz_recv, at_z(z_peer(i))).start())

    dec.gathered_x()
    sumdec[...] = (rxdec[0] + rxdec[1]) + (rxdec[2] + rxdec[3])
    dec.scatter_z()

    sz_all = all_of(sz, NZ, sz_send, sz_recv, at_z(z_peer(1)))
    sz_all.wait_recv()
    lse2, delta2 = merge_stats(sz, NZ)
    enc.gathered_x()
    factors = [jnp.exp(sx[i, 0:2, :] - lse2) for i in range(nx)]
    shifts = [sx[i, 2:4, :] - delta2 for i in range(nx)]
    for j in range(NZ):
        half = slice(j % 2, j % 2 + 1)
        terms = [
            factors[i][half] * (rxq[i, j, 0:4, :] + shifts[i][half] * rxq[i, j, 4:8, :])
            for i in range(nx)
        ]
        sumq[j] = functools.reduce(jnp.add, terms)
    enc.scatter_z()

    lse = jnp.concatenate([lse2[0:1], lse2[1:2]], axis=1)
    delta = jnp.concatenate([delta2[0:1], delta2[1:2]], axis=1)

    def enc_packets(i, carry):
        span = pl.ds(pl.multiple_of(i * size, size), size)
        p = expo[span, :] * jnp.exp(chunk_top[i] - lse)
        ds = (p * (edot[span, :] - delta)).astype(BF16)
        gpk_ref[span, :] = (dot(ds, lat_query, NN) * scale).astype(BF16)
        gpv_ref[span, :] = dot(p.astype(BF16), enc_grad, NN).astype(BF16)
        return carry

    lax.fori_loop(0, chunks // 2, enc_packets, 0)
    dec.gather_z()
    enc.gather_z()
    lax.fori_loop(chunks // 2, chunks, enc_packets, 0)
    dec.gather_x()
    enc.gather_x()
    dec.finish()
    glk_ref[...] = (fulldec[0:nx // 2].reshape(LAT, DH) * scale).astype(BF16)
    glv_ref[...] = fulldec[nx // 2:nx].reshape(LAT, DH)
    enc.finish()
    for i in range(nx):
        for k in range(0, NZ, 4):
            for c in range(2):
                at, lanes = place(i, k + c)
                query_t[at.start:at.start + 8, lanes] = jnp.concatenate(
                    [fullq[i, k + c], fullq[i, k + 2 + c]], axis=0
                )
    glq_ref[...] = (query_t[...].T * scale).astype(BF16)

    mask_all.wait_send()
    sx_all.wait_send()
    sz_all.wait_send()
    dec.drain()
    enc.drain()


def write_out(*refs):
    count = len(refs) // 2
    sems = refs[-1]
    copies = [
        pltpu.make_async_copy(refs[i], refs[count + i], sems.at[i]) for i in range(count)
    ]
    for copy in copies:
        copy.start()
    for copy in copies:
        copy.wait()


def solution(mesh):
    nx = mesh.shape["seq"] // NZ
    nh = mesh.shape["head"]

    def on_device(lq, pk, pv, eg, pq, lk, lv, dg, mask):
        rows = pk.shape[0]
        vmem = pl.BlockSpec(memory_space=pltpu.VMEM)
        hbm = pl.BlockSpec(memory_space=pltpu.HBM)
        lat = jax.ShapeDtypeStruct((LAT, DH), BF16)
        pkt = jax.ShapeDtypeStruct((rows, DH), BF16)
        outs = (lat, pkt, pkt, pkt, lat, jax.ShapeDtypeStruct((LAT, DH), F32))
        args = [
            pltpu.with_memory_space_constraint(x, pltpu.HBM)
            for x in (lq, pk, pv, eg, pq, lk, lv, dg, mask)
        ]

        def reduce_buffers(sent, depth):
            return [
                pltpu.VMEM((nx, NZ, sent, 128), F32),
                pltpu.VMEM((nx, NZ, sent, 128), F32),
                pltpu.VMEM((NZ, depth, 128), F32),
                pltpu.VMEM((NZ, depth, 128), F32),
                pltpu.VMEM((nx, NZ, depth, 128), F32),
            ]

        made = pl.pallas_call(
            functools.partial(kernel, nx, nh, rows),
            out_shape=outs,
            in_specs=[hbm] * len(args),
            out_specs=(vmem,) * len(outs),
            scratch_shapes=[pltpu.VMEM(x.shape, x.dtype) for x in args]
            + [
                pltpu.VMEM((nh, 1, 384), F32),
                pltpu.VMEM((rows, 128), F32),
                pltpu.VMEM((rows, LAT), F32),
                pltpu.VMEM((rows, LAT), F32),
                pltpu.VMEM((4, 1, LAT), F32),
                pltpu.VMEM((rows, LAT), F32),
                pltpu.VMEM((DH, LAT), F32),
                pltpu.VMEM((nx, 4, 128), F32),
                pltpu.VMEM((NZ, 4, 128), F32),
            ]
            + reduce_buffers(8, 8)
            + reduce_buffers(8, 4)
            + [pltpu.SemaphoreType.DMA((len(args),))]
            + [pltpu.SemaphoreType.DMA((1,))] * 22,
            compiler_params=pltpu.CompilerParams(
                collective_id=0, has_side_effects=True, vmem_limit_bytes=48 * 2**20
            ),
            name="perceiver_backward",
        )(*args)
        return pl.pallas_call(
            write_out,
            out_shape=outs,
            in_specs=[vmem] * len(outs),
            out_specs=(hbm,) * len(outs),
            scratch_shapes=[pltpu.SemaphoreType.DMA((len(outs),))],
            name="write_out",
        )(*made)

    return jax.shard_map(
        on_device,
        mesh=mesh,
        in_specs=(
            P(None, "head"),
            P("seq", "head"),
            P("seq", "head"),
            P(None, "head"),
            P("seq", "head"),
            P(None, "head"),
            P(None, "head"),
            P("seq", "head"),
            P(("seq", "head")),
        ),
        out_specs=(
            P(None, "head"),
            P("seq", "head"),
            P("seq", "head"),
            P("seq", "head"),
            P(None, "head"),
            P(None, "head"),
        ),
        check_vma=False,
    )
```

time: 569 us -> 62 us (0.11)
  the two profiles are of different devices: /device:TPU:24 before, /device:TPU:8 now
where the time goes in v1:
time: 62 us; the launch traced here: 61.9 us
  Pallas kernels  56.8 us (92%)
  local copies, waits for them, and re-layouts  4.4 us (7%)
  between operations  0.66 us (1%)
    pallas_call x1, Pallas kernels, on_device(): pl.pallas_call(functools.partial(kernel, nx, nh, rows), out_shape=outs, i...  54 us
    unnamed x12, local copies, waits for them, and re-layouts  4.4 us
    pallas_call x1, Pallas kernels, on_device(): pl.pallas_call(write_out, out_shape=outs, in_specs=[vmem] * len(outs), ou...  2.81 us

profile of v1, /device:TPU:8, one launch (start us, length us, event | category | flops | bytes accessed | tf_op | source)
XLA Modules:
  0.0 61.9 jit_solution(707699938779659265)
XLA Ops:
  0.6 54.0 %perceiver_backward.1 = (bf16[256,128]{1,0:T(8,128)(2,1)S(1)}, bf16[2304,128]{1,0:T(8,128)(2,1)S(1)}, bf16[2304,128]{1,0:T(8,128)(2,1)S(1)}, bf16[2304,128]{1,0:...) custom-call(bf16[256,128]{1,0:T(8,128)(2,1)} %lq_hbm.1, bf16[2304,128]{1,0:T(8,128)(2,1)} %pk_hbm.1, ...), custom_call_target="tpu_custom_call" | custom-call | tf_op jit(solution)/shard_map/perceiver_backward/pallas_call | solution.py:391
  54.7 0.0 copy-start
  54.7 0.8 %copy-done = bf16[2304,128]{1,0:T(8,128)(2,1)} copy-done((bf16[2304,128]{1,0:T(8,128)(2,1)}, bf16[2304,128]{1,0:T(8,128)(2,1)S(1)}, u32[]{:S(2)}) %copy-start) | copy-done | bytes 589848
  55.5 0.0 copy-start.1
  55.5 0.8 %copy-done.1 = bf16[2304,128]{1,0:T(8,128)(2,1)} copy-done((bf16[2304,128]{1,0:T(8,128)(2,1)}, bf16[2304,128]{1,0:T(8,128)(2,1)S(1)}, u32[]{:S(2)}) %copy-start.1) | copy-done | bytes 589848
  56.3 0.0 copy-start.2
  56.3 0.9 %copy-done.2 = bf16[2304,128]{1,0:T(8,128)(2,1)} copy-done((bf16[2304,128]{1,0:T(8,128)(2,1)}, bf16[2304,128]{1,0:T(8,128)(2,1)S(1)}, u32[]{:S(2)}) %copy-start.2) | copy-done | bytes 589848
  57.2 0.0 copy-start.3
  57.2 0.7 %copy-done.3 = f32[256,128]{1,0:T(8,128)} copy-done((f32[256,128]{1,0:T(8,128)}, f32[256,128]{1,0:T(8,128)S(1)}, u32[]{:S(2)}) %copy-start.3) | copy-done | bytes 131096
  57.8 0.0 copy-start.4
  57.8 0.6 %copy-done.4 = bf16[256,128]{1,0:T(8,128)(2,1)} copy-done((bf16[256,128]{1,0:T(8,128)(2,1)}, bf16[256,128]{1,0:T(8,128)(2,1)S(1)}, u32[]{:S(2)}) %copy-start.4) | copy-done | bytes 65560
  58.4 0.0 copy-start.5
  58.4 0.6 %copy-done.5 = bf16[256,128]{1,0:T(8,128)(2,1)} copy-done((bf16[256,128]{1,0:T(8,128)(2,1)}, bf16[256,128]{1,0:T(8,128)(2,1)S(1)}, u32[]{:S(2)}) %copy-start.5) | copy-done | bytes 65560
  59.1 2.8 %write_out.1 = (bf16[256,128]{1,0:T(8,128)(2,1)}, bf16[2304,128]{1,0:T(8,128)(2,1)}, bf16[2304,128]{1,0:T(8,128)(2,1)}, bf16[2304,128]{1,0:T(8,128)(2,1)}, bf16[256,128]{1,0:T(8,128)(2,1)}, /*index=5*/f32[256,128]{1,0:T(8,128)}) custom-call(bf16[256,128]{1,0:T(8,128)(2,1)} %copy-done.4, bf16[2304,128]{1,0:T(8,128)(2,1)} %copy-done, ...), custom_call_target="tpu_custom_call" | custom-call | tf_op jit(solution)/shard_map/write_out/pallas_call | solution.py:417
Async XLA Ops:
  54.7 0.8 %copy-start = (bf16[2304,128]{1,0:T(8,128)(2,1)}, bf16[2304,128]{1,0:T(8,128)(2,1)S(1)}, u32[]{:S(2)}) copy-start(bf16[2304,128]{1,0:T(8,128)(2,1)S(1)} %get-tuple-element.13.refs_1_) | copy-start | bytes 1769476
  55.5 0.8 %copy-start.1 = (bf16[2304,128]{1,0:T(8,128)(2,1)}, bf16[2304,128]{1,0:T(8,128)(2,1)S(1)}, u32[]{:S(2)}) copy-start(bf16[2304,128]{1,0:T(8,128)(2,1)S(1)} %get-tuple-element.14.refs_2_) | copy-start | bytes 1769476
  56.3 0.9 %copy-start.2 = (bf16[2304,128]{1,0:T(8,128)(2,1)}, bf16[2304,128]{1,0:T(8,128)(2,1)S(1)}, u32[]{:S(2)}) copy-start(bf16[2304,128]{1,0:T(8,128)(2,1)S(1)} %get-tuple-element.15.refs_3_) | copy-start | bytes 1769476
  57.2 0.7 %copy-start.3 = (f32[256,128]{1,0:T(8,128)}, f32[256,128]{1,0:T(8,128)S(1)}, u32[]{:S(2)}) copy-start(f32[256,128]{1,0:T(8,128)S(1)} %get-tuple-element.17.refs_5_) | copy-start | bytes 393220
  57.8 0.6 %copy-start.4 = (bf16[256,128]{1,0:T(8,128)(2,1)}, bf16[256,128]{1,0:T(8,128)(2,1)S(1)}, u32[]{:S(2)}) copy-start(bf16[256,128]{1,0:T(8,128)(2,1)S(1)} %get-tuple-element.12.refs_0_) | copy-start | bytes 196612
  58.4 0.6 %copy-start.5 = (bf16[256,128]{1,0:T(8,128)(2,1)}, bf16[256,128]{1,0:T(8,128)(2,1)S(1)}, u32[]{:S(2)}) copy-start(bf16[256,128]{1,0:T(8,128)(2,1)S(1)} %get-tuple-element.16.refs_4_) | copy-start | bytes 196612

commit v2 on v1

--- a/solution.py
+++ b/solution.py
@@ -41,7 +41,7 @@
     lq_hbm, pk_hbm, pv_hbm, eg_hbm, pq_hbm, lk_hbm, lv_hbm, dg_hbm, mask_hbm,
     glq_ref, gpk_ref, gpv_ref, gpq_ref, glk_ref, glv_ref,
     lq_ref, pk_ref, pv_ref, eg_ref, pq_ref, lk_ref, lv_ref, dg_ref, mask_ref,
-    maskbuf, mcol, expo, edot, chunk_top, dprob, query_t,
+    maskbuf, mcol, expo, edot, esums, dprob, dscore, query_t,
     sx, sz, pdec, rxdec, sumdec, rzdec, fulldec, pq, rxq, sumq, rzq, fullq,
     in_sems,
     m_send, m_recv, sx_send, sx_recv, sz_send, sz_recv,
@@ -50,8 +50,8 @@
 ):
     scale = 1.0 / math.sqrt(DH)
     piece = rows // nh
-    chunks = 4
-    size = rows // chunks
+    size = 384
+    spans = [slice(at, at + size) for at in range(0, rows, size)]
     seq = lax.axis_index("seq")
     head = lax.axis_index("head")
     xi = seq // NZ
@@ -132,46 +132,24 @@
         maskbuf.at[head], maskbuf.at[head], m_send, m_recv, at_head(head_peer(i))
     ).start())
 
-    loads[1].wait()
-    loads[2].wait()
+    for load in loads[1:5]:
+        load.wait()
     lat_key = lk_ref[...]
-
-    def dec_probs(i, carry):
-        span = pl.ds(pl.multiple_of(i * size, size), size)
-        score = dot(pq_ref[span, :], lat_key, NT) * scale
-        e = jnp.exp(score - jnp.max(score, axis=1, keepdims=True))
-        dprob[span, :] = e * (1.0 / jnp.sum(e, axis=1, keepdims=True))
-        return carry
-
-    lax.fori_loop(0, chunks, dec_probs, 0)
+    lat_value = lv_ref[...]
+    for span in spans:
+        score = dot(lat_key, pq_ref[span, :], NT) * scale
+        e = jnp.exp(score - jnp.max(score, axis=0, keepdims=True))
+        p = e * (1.0 / jnp.sum(e, axis=0, keepdims=True))
+        dg = dot(lat_value, dg_ref[span, :], NT)
+        dd = jnp.sum(p * dg, axis=0, keepdims=True)
+        dprob[:, span] = p.astype(BF16)
+        dscore[:, span] = (p * (dg - dd)).astype(BF16)
 
     mask_all = all_of(maskbuf, nh, m_send, m_recv, at_head(head_peer(1)))
     mask_all.wait_recv()
     for h in range(nh):
         line = jnp.broadcast_to(maskbuf[h], (128, 384))
         mcol[h * piece:(h + 1) * piece, :] = line.T[:piece, :]
-
-    loads[3].wait()
-    loads[4].wait()
-    lat_value = lv_ref[...]
-
-    def dec_grads(i, carry):
-        span = pl.ds(pl.multiple_of(i * size, size), size)
-        masked = dg_ref[span, :] * mcol[span, :].astype(BF16)
-        dg = dot(masked, lat_value, NT)
-        p = dprob[span, :]
-        dd = jnp.sum(p * dg, axis=1, keepdims=True)
-        ds = (p * (dg - dd)).astype(BF16)
-        gpq_ref[span, :] = (dot(ds, lat_key, NN) * scale).astype(BF16)
-        key_t, value_t = carry
-        key_t = key_t + dot(pq_ref[span, :], ds, TN)
-        value_t = value_t + dot(masked, p.astype(BF16), TN)
-        return key_t, value_t
-
-    blank = jnp.zeros((DH, LAT), F32)
-    key_t, value_t = lax.fori_loop(0, chunks, dec_grads, (blank, blank))
-    pdec[0:nx // 2] = key_t.T.reshape(nx // 2, NZ, 8, 128)
-    pdec[nx // 2:nx] = value_t.T.reshape(nx // 2, NZ, 8, 128)
 
     class Sum:
         def __init__(self, part, rx, summed, rz, full, *sems):
@@ -231,44 +209,33 @@
         pq, rxq, sumq, rzq, fullq,
         qx_send, qx_recv, qz_send, qz_recv, qaz_send, qaz_recv, qax_send, qax_recv,
     )
-    dec.scatter_x()
-
     for load in loads[5:]:
         load.wait()
     lat_query = lq_ref[...]
     enc_grad = eg_ref[...]
-
-    def enc_first(i, carry):
-        top, total, delta, a, b = carry
-        span = pl.ds(pl.multiple_of(i * size, size), size)
-        keys = pk_ref[span, :]
+    tops, totals, deltas = [], [], []
+    for span in spans:
         bias = (mcol[span, :] - 1.0) * 1e30
-        score = dot(keys, lat_query, NT) * scale
+        score = dot(pk_ref[span, :], lat_query, NT) * scale
         score = score + jnp.concatenate([bias, bias], axis=1)
         grad = dot(pv_ref[span, :], enc_grad, NT)
         own = jnp.max(score, axis=0, keepdims=True)
         e = jnp.exp(score - own)
         expo[span, :] = e
         edot[span, :] = grad
-        chunk_top[i] = own
         own_total = jnp.sum(e, axis=0, keepdims=True)
         own_delta = jnp.sum(e * grad, axis=0, keepdims=True) / own_total
-        ds = (e * (grad - own_delta)).astype(BF16)
-        sums = dot(keys, jnp.concatenate([ds, e.astype(BF16)], axis=1), TN)
-        own_a, own_b = sums[:, :LAT], sums[:, LAT:]
-        later = jnp.maximum(top, own)
-        left = jnp.exp(top - later)
-        right = jnp.exp(own - later)
-        both = total * left + own_total * right
-        mixed = (total * left * delta + own_total * right * own_delta) / both
-        a = left * (a + (delta - mixed) * b) + right * (own_a + (own_delta - mixed) * own_b)
-        b = left * b + right * own_b
-        return later, both, mixed, a, b
-
-    zero = jnp.zeros((1, LAT), F32)
-    top, total, delta, a, b = lax.fori_loop(
-        0, chunks, enc_first, (jnp.full((1, LAT), -3e30, F32), zero, zero, blank, blank)
-    )
+        esums[span, :LAT] = (e * (grad - own_delta)).astype(BF16)
+        esums[span, LAT:] = e.astype(BF16)
+        tops.append(own)
+        totals.append(own_total)
+        deltas.append(own_delta)
+    top = functools.reduce(jnp.maximum, tops)
+    shares = [jnp.exp(own - top) for own in tops]
+    weights = [w * t for w, t in zip(shares, totals)]
+    total = functools.reduce(jnp.add, weights)
+    inverse = 1.0 / total
+    delta = functools.reduce(jnp.add, [w * d for w, d in zip(weights, deltas)]) * inverse
 
     def put_stats(ref, slot, lse_rows, delta_rows):
         ref[slot, 0:2, :] = lse_rows
@@ -277,9 +244,28 @@
     put_stats(sx, xi, fold(top + jnp.log(total)), fold(delta))
     every(nx, lambda i: send(sx.at[xi], sx.at[xi], sx_send, sx_recv, at_x(x_peer(i))).start())
 
-    share = 1.0 / total
-    a = a * share
-    b = b * share
+    key_sum = jnp.zeros((LAT, DH), F32)
+    value_sum = jnp.zeros((LAT, DH), F32)
+    for span in spans:
+        valid = mcol[span, :].astype(BF16)
+        key_sum = key_sum + dot(dscore[:, span], pq_ref[span, :] * valid, NN)
+        value_sum = value_sum + dot(dprob[:, span], dg_ref[span, :] * valid, NN)
+    pdec[0:nx // 2] = key_sum.reshape(nx // 2, NZ, 8, 128)
+    pdec[nx // 2:nx] = value_sum.reshape(nx // 2, NZ, 8, 128)
+    dec.scatter_x()
+
+    sx_all = all_of(sx, nx, sx_send, sx_recv, at_x(x_peer(1)))
+    sx_all.wait_recv()
+    put_stats(sz, zi, *merge_stats(sx, nx))
+    every(NZ, lambda i: send(sz.at[zi], sz.at[zi], sz_send, sz_recv, at_z(z_peer(i))).start())
+
+    a = jnp.zeros((DH, LAT), F32)
+    b = jnp.zeros((DH, LAT), F32)
+    for span, w, d in zip(spans, shares, deltas):
+        sums = dot(pk_ref[span, :], esums[span, :], TN)
+        w = w * inverse
+        a = a + w * (sums[:, :LAT] + (d - delta) * sums[:, LAT:])
+        b = b + w * sums[:, LAT:]
 
     def place(i, j):
         at = i * (DH // nx) + (j // 2) * 4
@@ -290,10 +276,9 @@
             pq[i, j] = jnp.concatenate([a[place(i, j)], b[place(i, j)]], axis=0)
     enc.scatter_x()
 
-    sx_all = all_of(sx, nx, sx_send, sx_recv, at_x(x_peer(1)))
-    sx_all.wait_recv()
-    put_stats(sz, zi, *merge_stats(sx, nx))
-    every(NZ, lambda i: send(sz.at[zi], sz.at[zi], sz_send, sz_recv, at_z(z_peer(i))).start())
+    for span in spans:
+        grad = dot(dscore[:, span], lat_key, TN) * (mcol[span, :] * scale)
+        gpq_ref[span, :] = grad.astype(BF16)
 
     dec.gathered_x()
     sumdec[...] = (rxdec[0] + rxdec[1]) + (rxdec[2] + rxdec[3])
@@ -317,18 +302,17 @@
     lse = jnp.concatenate([lse2[0:1], lse2[1:2]], axis=1)
     delta = jnp.concatenate([delta2[0:1], delta2[1:2]], axis=1)
 
-    def enc_packets(i, carry):
-        span = pl.ds(pl.multiple_of(i * size, size), size)
-        p = expo[span, :] * jnp.exp(chunk_top[i] - lse)
-        ds = (p * (edot[span, :] - delta)).astype(BF16)
-        gpk_ref[span, :] = (dot(ds, lat_query, NN) * scale).astype(BF16)
-        gpv_ref[span, :] = dot(p.astype(BF16), enc_grad, NN).astype(BF16)
-        return carry
-
-    lax.fori_loop(0, chunks // 2, enc_packets, 0)
+    def enc_packets(first, last):
+        for span, own in zip(spans[first:last], tops[first:last]):
+            p = expo[span, :] * jnp.exp(own - lse)
+            ds = (p * (edot[span, :] - delta)).astype(BF16)
+            gpk_ref[span, :] = (dot(ds, lat_query, NN) * scale).astype(BF16)
+            gpv_ref[span, :] = dot(p.astype(BF16), enc_grad, NN).astype(BF16)
+
+    enc_packets(0, 3)
     dec.gather_z()
+    enc_packets(3, len(spans))
     enc.gather_z()
-    lax.fori_loop(chunks // 2, chunks, enc_packets, 0)
     dec.gather_x()
     enc.gather_x()
     dec.finish()
@@ -399,8 +383,9 @@
                 pltpu.VMEM((rows, 128), F32),
                 pltpu.VMEM((rows, LAT), F32),
                 pltpu.VMEM((rows, LAT), F32),
-                pltpu.VMEM((4, 1, LAT), F32),
-                pltpu.VMEM((rows, LAT), F32),
+                pltpu.VMEM((rows, 2 * LAT), BF16),
+                pltpu.VMEM((LAT, rows), BF16),
+                pltpu.VMEM((LAT, rows), BF16),
                 pltpu.VMEM((DH, LAT), F32),
                 pltpu.VMEM((nx, 4, 128), F32),
                 pltpu.VMEM((NZ, 4, 128), F32),
@@ -420,8 +405,9 @@
             in_specs=[vmem] * len(outs),
             out_specs=(hbm,) * len(outs),
             scratch_shapes=[pltpu.SemaphoreType.DMA((len(outs),))],
+            compiler_params=pltpu.CompilerParams(vmem_limit_bytes=2**20),
             name="write_out",
-        )(*made)
+        )(*[pltpu.with_memory_space_constraint(x, pltpu.VMEM) for x in made])
 
     return jax.shard_map(
         on_device,

time: 62 us -> 51.5 us (0.83)
  the two profiles are of different devices: /device:TPU:8 before, /device:TPU:32 now
where the time goes in v2:
time: 51.5 us; the launch traced here: 51.3 us
  Pallas kernels  50.7 us (98%)
  between operations  0.64 us (1%)
    pallas_call x1, Pallas kernels, on_device(): pl.pallas_call(functools.partial(kernel, nx, nh, rows), out_shape=outs, i...  49.4 us
    pallas_call x1, Pallas kernels, on_device(): pl.pallas_call(write_out, out_shape=outs, in_specs=[vmem] * len(outs), ou...  1.34 us

profile of v2, /device:TPU:32, one launch (start us, length us, event | category | flops | bytes accessed | tf_op | source)
XLA Modules:
  0.0 51.3 jit_solution(10671280904957014668)
XLA Ops:
  0.6 49.4 %perceiver_backward.1 = (bf16[256,128]{1,0:T(8,128)(2,1)S(1)}, bf16[2304,128]{1,0:T(8,128)(2,1)S(1)}, bf16[2304,128]{1,0:T(8,128)(2,1)S(1)}, bf16[2304,128]{1,0:...) custom-call(bf16[256,128]{1,0:T(8,128)(2,1)} %lq_hbm.1, bf16[2304,128]{1,0:T(8,128)(2,1)} %pk_hbm.1, ...), custom_call_target="tpu_custom_call" | custom-call | tf_op jit(solution)/shard_map/perceiver_backward/pallas_call | solution.py:375
  50.0 1.3 %write_out.1 = (bf16[256,128]{1,0:T(8,128)(2,1)}, bf16[2304,128]{1,0:T(8,128)(2,1)}, bf16[2304,128]{1,0:T(8,128)(2,1)}, bf16[2304,128]{1,0:T(8,128)(2,1)}, bf16[256,128]{1,0:T(8,128)(2,1)}, /*index=5*/f32[256,128]{1,0:T(8,128)}) custom-call(bf16[256,128]{1,0:T(8,128)(2,1)S(1)} %get-tuple-element.12.refs_0_, bf16[2304,128]{1,0:T(8,128)(2,1)S(1)} %get-tuple-element.13.refs_1_, ...), custom_call_target="tpu_custom_call" | custom-call | tf_op jit(solution)/shard_map/write_out/pallas_call | solution.py:402

commit v3 on v2

--- a/solution.py
+++ b/solution.py
@@ -30,6 +30,12 @@
     total = functools.reduce(jnp.add, weights)
     mixed = functools.reduce(jnp.add, [w * ref[i, 2:4, :] for i, w in enumerate(weights)])
     return top + jnp.log(total), mixed / total
+
+
+def tree_sum(pieces):
+    while len(pieces) > 1:
+        pieces = [a + b for a, b in zip(pieces[0::2], pieces[1::2])]
+    return pieces[0]
 
 
 def fold(line):
@@ -126,17 +132,20 @@
     loads[0].wait()
     maskbuf[head] = jnp.zeros((1, 384), F32)
     maskbuf[head, :, 0:piece] = (mask_ref[...] > 0).astype(F32).reshape(1, piece)
-    pl.semaphore_wait(barrier, nh + nx + NZ - 3)
-
-    every(nh, lambda i: send(
-        maskbuf.at[head], maskbuf.at[head], m_send, m_recv, at_head(head_peer(i))
-    ).start())
+    def start_masks():
+        pl.semaphore_wait(barrier, nh + nx + NZ - 3)
+
+        every(nh, lambda i: send(
+            maskbuf.at[head], maskbuf.at[head], m_send, m_recv, at_head(head_peer(i))
+        ).start())
 
     for load in loads[1:5]:
         load.wait()
     lat_key = lk_ref[...]
     lat_value = lv_ref[...]
-    for span in spans:
+    for at, span in enumerate(spans):
+        if at == len(spans) // 2:
+            start_masks()
         score = dot(lat_key, pq_ref[span, :], NT) * scale
         e = jnp.exp(score - jnp.max(score, axis=0, keepdims=True))
         p = e * (1.0 / jnp.sum(e, axis=0, keepdims=True))
@@ -177,13 +186,10 @@
                 self.summed.at[z_peer(i)], self.rz.at[zi], *self.z_sems, at_z(z_peer(i))
             ).start())
 
-        def gather_z(self):
+        def gather_z(self, join):
             self.rz[zi] = self.summed[zi]
             self.whole[1].wait_recv()
-            pieces = [self.rz[i] for i in range(NZ)]
-            while len(pieces) > 1:
-                pieces = [a + b for a, b in zip(pieces[0::2], pieces[1::2])]
-            self.full[xi, zi] = pieces[0]
+            self.full[xi, zi] = join([self.rz[i] for i in range(NZ)])
             every(NZ, lambda i: send(
                 self.full.at[xi, zi], self.full.at[xi, zi], *self.az_sems, at_z(z_peer(i))
             ).start())
@@ -209,6 +215,16 @@
         pq, rxq, sumq, rzq, fullq,
         qx_send, qx_recv, qz_send, qz_recv, qaz_send, qaz_recv, qax_send, qax_recv,
     )
+    key_sum = jnp.zeros((LAT, DH), F32)
+    value_sum = jnp.zeros((LAT, DH), F32)
+    for span in spans:
+        valid = mcol[span, :].astype(BF16)
+        key_sum = key_sum + dot(dscore[:, span], pq_ref[span, :] * valid, NN)
+        value_sum = value_sum + dot(dprob[:, span], dg_ref[span, :] * valid, NN)
+    pdec[0:nx // 2] = key_sum.reshape(nx // 2, NZ, 8, 128)
+    pdec[nx // 2:nx] = value_sum.reshape(nx // 2, NZ, 8, 128)
+    dec.scatter_x()
+
     for load in loads[5:]:
         load.wait()
     lat_query = lq_ref[...]
@@ -244,20 +260,9 @@
     put_stats(sx, xi, fold(top + jnp.log(total)), fold(delta))
     every(nx, lambda i: send(sx.at[xi], sx.at[xi], sx_send, sx_recv, at_x(x_peer(i))).start())
 
-    key_sum = jnp.zeros((LAT, DH), F32)
-    value_sum = jnp.zeros((LAT, DH), F32)
-    for span in spans:
-        valid = mcol[span, :].astype(BF16)
-        key_sum = key_sum + dot(dscore[:, span], pq_ref[span, :] * valid, NN)
-        value_sum = value_sum + dot(dprob[:, span], dg_ref[span, :] * valid, NN)
-    pdec[0:nx // 2] = key_sum.reshape(nx // 2, NZ, 8, 128)
-    pdec[nx // 2:nx] = value_sum.reshape(nx // 2, NZ, 8, 128)
-    dec.scatter_x()
-
-    sx_all = all_of(sx, nx, sx_send, sx_recv, at_x(x_peer(1)))
-    sx_all.wait_recv()
-    put_stats(sz, zi, *merge_stats(sx, nx))
-    every(NZ, lambda i: send(sz.at[zi], sz.at[zi], sz_send, sz_recv, at_z(z_peer(i))).start())
+    dec.gathered_x()
+    sumdec[...] = (rxdec[0] + rxdec[1]) + (rxdec[2] + rxdec[3])
+    dec.scatter_z()
 
     a = jnp.zeros((DH, LAT), F32)
     b = jnp.zeros((DH, LAT), F32)
@@ -276,31 +281,56 @@
             pq[i, j] = jnp.concatenate([a[place(i, j)], b[place(i, j)]], axis=0)
     enc.scatter_x()
 
+    sx_all = all_of(sx, nx, sx_send, sx_recv, at_x(x_peer(1)))
+    sx_all.wait_recv()
+    lse_x, delta_x = merge_stats(sx, nx)
+    put_stats(sz, zi, lse_x, delta_x)
+    every(NZ, lambda i: send(sz.at[zi], sz.at[zi], sz_send, sz_recv, at_z(z_peer(i))).start())
+
     for span in spans:
         grad = dot(dscore[:, span], lat_key, TN) * (mcol[span, :] * scale)
         gpq_ref[span, :] = grad.astype(BF16)
 
-    dec.gathered_x()
-    sumdec[...] = (rxdec[0] + rxdec[1]) + (rxdec[2] + rxdec[3])
-    dec.scatter_z()
+    dec.gather_z(tree_sum)
+
+    def combine(factors, shifts, sums):
+        a = functools.reduce(
+            jnp.add, [f * (s[0:4] + d * s[4:8]) for f, d, s in zip(factors, shifts, sums)]
+        )
+        return a, functools.reduce(jnp.add, [f * s[4:8] for f, s in zip(factors, sums)])
+
+    enc.gathered_x()
+    factors = [jnp.exp(sx[i, 0:2, :] - lse_x) for i in range(nx)]
+    shifts = [sx[i, 2:4, :] - delta_x for i in range(nx)]
+    for j in range(NZ):
+        half = slice(j % 2, j % 2 + 1)
+        sumq[j] = jnp.concatenate(
+            combine(
+                [f[half] for f in factors],
+                [d[half] for d in shifts],
+                [rxq[i, j] for i in range(nx)],
+            ),
+            axis=0,
+        )
+    enc.scatter_z()
 
     sz_all = all_of(sz, NZ, sz_send, sz_recv, at_z(z_peer(1)))
     sz_all.wait_recv()
     lse2, delta2 = merge_stats(sz, NZ)
-    enc.gathered_x()
-    factors = [jnp.exp(sx[i, 0:2, :] - lse2) for i in range(nx)]
-    shifts = [sx[i, 2:4, :] - delta2 for i in range(nx)]
-    for j in range(NZ):
-        half = slice(j % 2, j % 2 + 1)
-        terms = [
-            factors[i][half] * (rxq[i, j, 0:4, :] + shifts[i][half] * rxq[i, j, 4:8, :])
-            for i in range(nx)
-        ]
-        sumq[j] = functools.reduce(jnp.add, terms)
-    enc.scatter_z()
-
     lse = jnp.concatenate([lse2[0:1], lse2[1:2]], axis=1)
     delta = jnp.concatenate([delta2[0:1], delta2[1:2]], axis=1)
+
+    def join_queries(sums):
+        own_half = lax.rem(zi, 2) == 0
+
+        def mine(lines):
+            return jnp.where(own_half, lines[0:1], lines[1:2])
+
+        return combine(
+            [mine(jnp.exp(sz[i, 0:2, :] - lse2)) for i in range(NZ)],
+            [mine(sz[i, 2:4, :] - delta2) for i in range(NZ)],
+            sums,
+        )[0]
 
     def enc_packets(first, last):
         for span, own in zip(spans[first:last], tops[first:last]):
@@ -310,10 +340,9 @@
             gpv_ref[span, :] = dot(p.astype(BF16), enc_grad, NN).astype(BF16)
 
     enc_packets(0, 3)
-    dec.gather_z()
+    dec.gather_x()
+    enc.gather_z(join_queries)
     enc_packets(3, len(spans))
-    enc.gather_z()
-    dec.gather_x()
     enc.gather_x()
     dec.finish()
     glk_ref[...] = (fulldec[0:nx // 2].reshape(LAT, DH) * scale).astype(BF16)
@@ -367,8 +396,8 @@
             return [
                 pltpu.VMEM((nx, NZ, sent, 128), F32),
                 pltpu.VMEM((nx, NZ, sent, 128), F32),
-                pltpu.VMEM((NZ, depth, 128), F32),
-                pltpu.VMEM((NZ, depth, 128), F32),
+                pltpu.VMEM((NZ, sent, 128), F32),
+                pltpu.VMEM((NZ, sent, 128), F32),
                 pltpu.VMEM((nx, NZ, depth, 128), F32),
             ]
 

time: 51.5 us -> 54.2 us (1.052)
  Pallas kernels: 50.7 us -> 53.5 us
    pallas_call x1, Pallas kernels: 49.4 us -> 52.1 us  [on_device(): pl.pallas_call(functools.partial(kernel, nx, nh, rows), out_shape=outs, i...]
where the time goes in v3:
time: 54.2 us; the launch traced here: 54.1 us
  Pallas kernels  53.5 us (99%)
  between operations  0.64 us (1%)
    pallas_call x1, Pallas kernels, on_device(): pl.pallas_call(functools.partial(kernel, nx, nh, rows), out_shape=outs, i...  52.1 us
    pallas_call x1, Pallas kernels, on_device(): pl.pallas_call(write_out, out_shape=outs, in_specs=[vmem] * len(outs), ou...  1.34 us

profile of v3, /device:TPU:32, one launch (start us, length us, event | category | flops | bytes accessed | tf_op | source)
XLA Modules:
  0.0 54.1 jit_solution(11813958534913625386)
XLA Ops:
  0.6 52.1 %perceiver_backward.1 = (bf16[256,128]{1,0:T(8,128)(2,1)S(1)}, bf16[2304,128]{1,0:T(8,128)(2,1)S(1)}, bf16[2304,128]{1,0:T(8,128)(2,1)S(1)}, bf16[2304,128]{1,0:...) custom-call(bf16[256,128]{1,0:T(8,128)(2,1)} %lq_hbm.1, bf16[2304,128]{1,0:T(8,128)(2,1)} %pk_hbm.1, ...), custom_call_target="tpu_custom_call" | custom-call | tf_op jit(solution)/shard_map/perceiver_backward/pallas_call | solution.py:404
  52.8 1.3 %write_out.1 = (bf16[256,128]{1,0:T(8,128)(2,1)}, bf16[2304,128]{1,0:T(8,128)(2,1)}, bf16[2304,128]{1,0:T(8,128)(2,1)}, bf16[2304,128]{1,0:T(8,128)(2,1)}, bf16[256,128]{1,0:T(8,128)(2,1)}, /*index=5*/f32[256,128]{1,0:T(8,128)}) custom-call(bf16[256,128]{1,0:T(8,128)(2,1)S(1)} %get-tuple-element.12.refs_0_, bf16[2304,128]{1,0:T(8,128)(2,1)S(1)} %get-tuple-element.13.refs_1_, ...), custom_call_target="tpu_custom_call" | custom-call | tf_op jit(solution)/shard_map/write_out/pallas_call | solution.py:431

commit v4 on v2

--- a/solution.py
+++ b/solution.py
@@ -42,6 +42,7 @@
     glq_ref, gpk_ref, gpv_ref, gpq_ref, glk_ref, glv_ref,
     lq_ref, pk_ref, pv_ref, eg_ref, pq_ref, lk_ref, lv_ref, dg_ref, mask_ref,
     maskbuf, mcol, expo, edot, esums, dprob, dscore, query_t,
+    tops_ref, totals_ref, deltas_ref,
     sx, sz, pdec, rxdec, sumdec, rzdec, fulldec, pq, rxq, sumq, rzq, fullq,
     in_sems,
     m_send, m_recv, sx_send, sx_recv, sz_send, sz_recv,
@@ -51,7 +52,16 @@
     scale = 1.0 / math.sqrt(DH)
     piece = rows // nh
     size = 384
-    spans = [slice(at, at + size) for at in range(0, rows, size)]
+    steps, unroll = rows // size // 2, 2
+
+    def chunks(first, last, body, carry=0):
+        def step(i, carry):
+            for k in range(unroll):
+                at = i * unroll + k
+                carry = body(at, pl.ds(pl.multiple_of(at * size, size), size), carry)
+            return carry
+
+        return lax.fori_loop(first, last, step, carry)
     seq = lax.axis_index("seq")
     head = lax.axis_index("head")
     xi = seq // NZ
@@ -136,7 +146,8 @@
         load.wait()
     lat_key = lk_ref[...]
     lat_value = lv_ref[...]
-    for span in spans:
+
+    def dec_chunk(at, span, carry):
         score = dot(lat_key, pq_ref[span, :], NT) * scale
         e = jnp.exp(score - jnp.max(score, axis=0, keepdims=True))
         p = e * (1.0 / jnp.sum(e, axis=0, keepdims=True))
@@ -144,6 +155,9 @@
         dd = jnp.sum(p * dg, axis=0, keepdims=True)
         dprob[:, span] = p.astype(BF16)
         dscore[:, span] = (p * (dg - dd)).astype(BF16)
+        return carry
+
+    chunks(0, steps, dec_chunk)
 
     mask_all = all_of(maskbuf, nh, m_send, m_recv, at_head(head_peer(1)))
     mask_all.wait_recv()
@@ -213,8 +227,8 @@
         load.wait()
     lat_query = lq_ref[...]
     enc_grad = eg_ref[...]
-    tops, totals, deltas = [], [], []
-    for span in spans:
+
+    def enc_chunk(at, span, carry):
         bias = (mcol[span, :] - 1.0) * 1e30
         score = dot(pk_ref[span, :], lat_query, NT) * scale
         score = score + jnp.concatenate([bias, bias], axis=1)
@@ -227,9 +241,16 @@
         own_delta = jnp.sum(e * grad, axis=0, keepdims=True) / own_total
         esums[span, :LAT] = (e * (grad - own_delta)).astype(BF16)
         esums[span, LAT:] = e.astype(BF16)
-        tops.append(own)
-        totals.append(own_total)
-        deltas.append(own_delta)
+        tops_ref[at] = own
+        totals_ref[at] = own_total
+        deltas_ref[at] = own_delta
+        return carry
+
+    chunks(0, steps, enc_chunk)
+    count = steps * unroll
+    tops = [tops_ref[i] for i in range(count)]
+    totals = [totals_ref[i] for i in range(count)]
+    deltas = [deltas_ref[i] for i in range(count)]
     top = functools.reduce(jnp.maximum, tops)
     shares = [jnp.exp(own - top) for own in tops]
     weights = [w * t for w, t in zip(shares, totals)]
@@ -244,12 +265,15 @@
     put_stats(sx, xi, fold(top + jnp.log(total)), fold(delta))
     every(nx, lambda i: send(sx.at[xi], sx.at[xi], sx_send, sx_recv, at_x(x_peer(i))).start())
 
-    key_sum = jnp.zeros((LAT, DH), F32)
-    value_sum = jnp.zeros((LAT, DH), F32)
-    for span in spans:
+    def dec_sums(at, span, carry):
         valid = mcol[span, :].astype(BF16)
+        key_sum, value_sum = carry
         key_sum = key_sum + dot(dscore[:, span], pq_ref[span, :] * valid, NN)
         value_sum = value_sum + dot(dprob[:, span], dg_ref[span, :] * valid, NN)
+        return key_sum, value_sum
+
+    blank = jnp.zeros((LAT, DH), F32)
+    key_sum, value_sum = chunks(0, steps, dec_sums, (blank, blank))
     pdec[0:nx // 2] = key_sum.reshape(nx // 2, NZ, 8, 128)
     pdec[nx // 2:nx] = value_sum.reshape(nx // 2, NZ, 8, 128)
     dec.scatter_x()
@@ -259,13 +283,17 @@
     put_stats(sz, zi, *merge_stats(sx, nx))
     every(NZ, lambda i: send(sz.at[zi], sz.at[zi], sz_send, sz_recv, at_z(z_peer(i))).start())
 
-    a = jnp.zeros((DH, LAT), F32)
-    b = jnp.zeros((DH, LAT), F32)
-    for span, w, d in zip(spans, shares, deltas):
+    def key_sums(at, span, carry):
+        a, b = carry
         sums = dot(pk_ref[span, :], esums[span, :], TN)
-        w = w * inverse
+        w = jnp.exp(tops_ref[at] - top) * inverse
+        d = deltas_ref[at]
         a = a + w * (sums[:, :LAT] + (d - delta) * sums[:, LAT:])
         b = b + w * sums[:, LAT:]
+        return a, b
+
+    blank = jnp.zeros((DH, LAT), F32)
+    a, b = chunks(0, steps, key_sums, (blank, blank))
 
     def place(i, j):
         at = i * (DH // nx) + (j // 2) * 4
@@ -276,9 +304,12 @@
             pq[i, j] = jnp.concatenate([a[place(i, j)], b[place(i, j)]], axis=0)
     enc.scatter_x()
 
-    for span in spans:
+    def dec_packets(at, span, carry):
         grad = dot(dscore[:, span], lat_key, TN) * (mcol[span, :] * scale)
         gpq_ref[span, :] = grad.astype(BF16)
+        return carry
+
+    chunks(0, steps, dec_packets)
 
     dec.gathered_x()
     sumdec[...] = (rxdec[0] + rxdec[1]) + (rxdec[2] + rxdec[3])
@@ -302,16 +333,16 @@
     lse = jnp.concatenate([lse2[0:1], lse2[1:2]], axis=1)
     delta = jnp.concatenate([delta2[0:1], delta2[1:2]], axis=1)
 
-    def enc_packets(first, last):
-        for span, own in zip(spans[first:last], tops[first:last]):
-            p = expo[span, :] * jnp.exp(own - lse)
-            ds = (p * (edot[span, :] - delta)).astype(BF16)
-            gpk_ref[span, :] = (dot(ds, lat_query, NN) * scale).astype(BF16)
-            gpv_ref[span, :] = dot(p.astype(BF16), enc_grad, NN).astype(BF16)
-
-    enc_packets(0, 3)
+    def enc_packets(at, span, carry):
+        p = expo[span, :] * jnp.exp(tops_ref[at] - lse)
+        ds = (p * (edot[span, :] - delta)).astype(BF16)
+        gpk_ref[span, :] = (dot(ds, lat_query, NN) * scale).astype(BF16)
+        gpv_ref[span, :] = dot(p.astype(BF16), enc_grad, NN).astype(BF16)
+        return carry
+
+    chunks(0, 1, enc_packets)
     dec.gather_z()
-    enc_packets(3, len(spans))
+    chunks(1, steps, enc_packets)
     enc.gather_z()
     dec.gather_x()
     enc.gather_x()
@@ -387,6 +418,9 @@
                 pltpu.VMEM((LAT, rows), BF16),
                 pltpu.VMEM((LAT, rows), BF16),
                 pltpu.VMEM((DH, LAT), F32),
+                pltpu.VMEM((6, 1, LAT), F32),
+                pltpu.VMEM((6, 1, LAT), F32),
+                pltpu.VMEM((6, 1, LAT), F32),
                 pltpu.VMEM((nx, 4, 128), F32),
                 pltpu.VMEM((NZ, 4, 128), F32),
             ]

time: 51.5 us -> 52.4 us (1.017)
  Pallas kernels: 50.7 us -> 51.6 us
    pallas_call x1, Pallas kernels: 49.4 us -> 50.3 us  [on_device(): pl.pallas_call(functools.partial(kernel, nx, nh, rows), out_shape=outs, i...]
where the time goes in v4:
time: 52.4 us; the launch traced here: 52.3 us
  Pallas kernels  51.6 us (98%)
  between operations  0.64 us (1%)
    pallas_call x1, Pallas kernels, on_device(): pl.pallas_call(functools.partial(kernel, nx, nh, rows), out_shape=outs, i...  50.3 us
    pallas_call x1, Pallas kernels, on_device(): pl.pallas_call(write_out, out_shape=outs, in_specs=[vmem] * len(outs), ou...  1.34 us

profile of v4, /device:TPU:32, one launch (start us, length us, event | category | flops | bytes accessed | tf_op | source)
XLA Modules:
  0.0 52.3 jit_solution(16460641563418982856)
XLA Ops:
  0.6 50.3 %perceiver_backward.1 = (bf16[256,128]{1,0:T(8,128)(2,1)S(1)}, bf16[2304,128]{1,0:T(8,128)(2,1)S(1)}, bf16[2304,128]{1,0:T(8,128)(2,1)S(1)}, bf16[2304,128]{1,0:...) custom-call(bf16[256,128]{1,0:T(8,128)(2,1)} %lq_hbm.1, bf16[2304,128]{1,0:T(8,128)(2,1)} %pk_hbm.1, ...), custom_call_target="tpu_custom_call" | custom-call | tf_op jit(solution)/shard_map/perceiver_backward/pallas_call | solution.py:406
  50.9 1.3 %write_out.1 = (bf16[256,128]{1,0:T(8,128)(2,1)}, bf16[2304,128]{1,0:T(8,128)(2,1)}, bf16[2304,128]{1,0:T(8,128)(2,1)}, bf16[2304,128]{1,0:T(8,128)(2,1)}, bf16[256,128]{1,0:T(8,128)(2,1)}, /*index=5*/f32[256,128]{1,0:T(8,128)}) custom-call(bf16[256,128]{1,0:T(8,128)(2,1)S(1)} %get-tuple-element.12.refs_0_, bf16[2304,128]{1,0:T(8,128)(2,1)S(1)} %get-tuple-element.13.refs_1_, ...), custom_call_target="tpu_custom_call" | custom-call | tf_op jit(solution)/shard_map/write_out/pallas_call | solution.py:436

commit v5 on v2

--- a/solution.py
+++ b/solution.py
@@ -11,6 +11,8 @@
 DH = 128
 LAT = 256
 NZ = 16
+NL = 4
+NH = NZ // NL
 MESH = pl.DeviceIdType.MESH
 F32 = jnp.float32
 BF16 = jnp.bfloat16
@@ -32,6 +34,12 @@
     return top + jnp.log(total), mixed / total
 
 
+def tree_sum(pieces):
+    while len(pieces) > 1:
+        pieces = [a + b for a, b in zip(pieces[0::2], pieces[1::2])]
+    return pieces[0]
+
+
 def fold(line):
     return jnp.concatenate([line[:, :128], line[:, 128:]], axis=0)
 
@@ -42,12 +50,14 @@
     glq_ref, gpk_ref, gpv_ref, gpq_ref, glk_ref, glv_ref,
     lq_ref, pk_ref, pv_ref, eg_ref, pq_ref, lk_ref, lv_ref, dg_ref, mask_ref,
     maskbuf, mcol, expo, edot, esums, dprob, dscore, query_t,
-    sx, sz, pdec, rxdec, sumdec, rzdec, fulldec, pq, rxq, sumq, rzq, fullq,
-    in_sems,
-    m_send, m_recv, sx_send, sx_recv, sz_send, sz_recv,
-    dx_send, dx_recv, dz_send, dz_recv, daz_send, daz_recv, dax_send, dax_recv,
-    qx_send, qx_recv, qz_send, qz_recv, qaz_send, qaz_recv, qax_send, qax_recv,
+    sx, sl, sh, *rest,
 ):
+    pdec, rxdec, sumdec, rldec, midec, rhdec, fulldec = rest[0:7]
+    pq, rxq, sumq, rlq, midq, rhq, fullq = rest[7:14]
+    in_sems = rest[14]
+    m_sems, sx_sems, sl_sems, sh_sems, *sum_sems = [
+        tuple(rest[i:i + 2]) for i in range(15, len(rest), 2)
+    ]
     scale = 1.0 / math.sqrt(DH)
     piece = rows // nh
     size = 384
@@ -56,6 +66,8 @@
     head = lax.axis_index("head")
     xi = seq // NZ
     zi = lax.rem(seq, NZ)
+    li = lax.rem(zi, NL)
+    hi = zi // NL
 
     loads = [
         pltpu.make_async_copy(src, dst, in_sems.at[i])
@@ -82,8 +94,11 @@
     def x_peer(step):
         return lax.rem(xi + step, nx)
 
-    def z_peer(step):
-        return lax.rem(zi + NZ // 2 + (step // 2) * (2 * lax.rem(step, 2) - 1), NZ)
+    def l_peer(step):
+        return lax.rem(li + step, NL)
+
+    def h_peer(step):
+        return lax.rem(hi + step, NH)
 
     def at_head(peer):
         return (seq, peer)
@@ -91,8 +106,11 @@
     def at_x(peer):
         return (peer * NZ + zi, head)
 
-    def at_z(peer):
-        return (xi * NZ + peer, head)
+    def at_l(peer):
+        return (xi * NZ + hi * NL + peer, head)
+
+    def at_h(peer):
+        return (xi * NZ + peer * NL + li, head)
 
     def every(count, body):
         def step(i, carry):
@@ -122,21 +140,24 @@
 
     every(nh, greet(head_peer, at_head))
     every(nx, greet(x_peer, at_x))
-    every(NZ, greet(z_peer, at_z))
+    every(NL, greet(l_peer, at_l))
+    every(NH, greet(h_peer, at_h))
     loads[0].wait()
     maskbuf[head] = jnp.zeros((1, 384), F32)
     maskbuf[head, :, 0:piece] = (mask_ref[...] > 0).astype(F32).reshape(1, piece)
-    pl.semaphore_wait(barrier, nh + nx + NZ - 3)
-
-    every(nh, lambda i: send(
-        maskbuf.at[head], maskbuf.at[head], m_send, m_recv, at_head(head_peer(i))
-    ).start())
+    def start_masks():
+        pl.semaphore_wait(barrier, nh + nx + NL + NH - 4)
+        every(nh, lambda i: send(
+            maskbuf.at[head], maskbuf.at[head], *m_sems, at_head(head_peer(i))
+        ).start())
 
     for load in loads[1:5]:
         load.wait()
     lat_key = lk_ref[...]
     lat_value = lv_ref[...]
-    for span in spans:
+    for at, span in enumerate(spans):
+        if at == len(spans) // 2:
+            start_masks()
         score = dot(lat_key, pq_ref[span, :], NT) * scale
         e = jnp.exp(score - jnp.max(score, axis=0, keepdims=True))
         p = e * (1.0 / jnp.sum(e, axis=0, keepdims=True))
@@ -145,70 +166,77 @@
         dprob[:, span] = p.astype(BF16)
         dscore[:, span] = (p * (dg - dd)).astype(BF16)
 
-    mask_all = all_of(maskbuf, nh, m_send, m_recv, at_head(head_peer(1)))
+    mask_all = all_of(maskbuf, nh, *m_sems, at_head(head_peer(1)))
     mask_all.wait_recv()
     for h in range(nh):
         line = jnp.broadcast_to(maskbuf[h], (128, 384))
         mcol[h * piece:(h + 1) * piece, :] = line.T[:piece, :]
 
     class Sum:
-        def __init__(self, part, rx, summed, rz, full, *sems):
-            self.part, self.rx, self.summed, self.rz, self.full = part, rx, summed, rz, full
-            self.x_sems, self.z_sems = sems[0:2], sems[2:4]
-            self.az_sems, self.ax_sems = sems[4:6], sems[6:8]
+        def __init__(self, part, rx, summed, rl, middle, rh, full, x, l, h, ah, al, ax):
+            self.part, self.rx, self.summed, self.rl = part, rx, summed, rl
+            self.middle, self.rh, self.full = middle, rh, full
+            self.x, self.l, self.h, self.ah, self.al, self.ax = x, l, h, ah, al, ax
+            self.own = full.at[xi, li]
             self.whole = [
-                all_of(rx, nx, *self.x_sems, at_x(x_peer(1))),
-                all_of(rz, NZ, *self.z_sems, at_z(z_peer(1))),
-                all_of(full.at[xi], NZ, *self.az_sems, at_z(z_peer(1))),
-                all_of(full, nx, *self.ax_sems, at_x(x_peer(1))),
+                all_of(rx, nx, *x, at_x(x_peer(1))),
+                all_of(rl, NL, *l, at_l(l_peer(1))),
+                all_of(rh, NH, *h, at_h(h_peer(1))),
+                all_of(self.own, NH, *ah, at_h(h_peer(1))),
+                all_of(full.at[xi], NL, *al, at_l(l_peer(1))),
+                all_of(full, nx, *ax, at_x(x_peer(1))),
             ]
 
         def scatter_x(self):
             every(nx, lambda i: send(
-                self.part.at[x_peer(i)], self.rx.at[xi], *self.x_sems, at_x(x_peer(i))
+                self.part.at[x_peer(i)], self.rx.at[xi], *self.x, at_x(x_peer(i))
             ).start())
 
         def gathered_x(self):
             self.rx[xi] = self.part[xi]
             self.whole[0].wait_recv()
 
-        def scatter_z(self):
-            every(NZ, lambda i: send(
-                self.summed.at[z_peer(i)], self.rz.at[zi], *self.z_sems, at_z(z_peer(i))
+        def scatter_l(self):
+            every(NL, lambda i: send(
+                self.summed.at[l_peer(i)], self.rl.at[li], *self.l, at_l(l_peer(i))
             ).start())
 
-        def gather_z(self):
-            self.rz[zi] = self.summed[zi]
+        def scatter_h(self):
+            self.rl[li] = self.summed[li]
             self.whole[1].wait_recv()
-            pieces = [self.rz[i] for i in range(NZ)]
-            while len(pieces) > 1:
-                pieces = [a + b for a, b in zip(pieces[0::2], pieces[1::2])]
-            self.full[xi, zi] = pieces[0]
-            every(NZ, lambda i: send(
-                self.full.at[xi, zi], self.full.at[xi, zi], *self.az_sems, at_z(z_peer(i))
+            self.middle[...] = tree_sum([self.rl[i] for i in range(NL)])
+            every(NH, lambda i: send(
+                self.middle.at[h_peer(i)], self.rh.at[hi], *self.h, at_h(h_peer(i))
             ).start())
 
+        def gather_h(self):
+            self.rh[hi] = self.middle[hi]
+            self.whole[2].wait_recv()
+            self.full[xi, li, hi] = tree_sum([self.rh[i] for i in range(NH)])
+            every(NH, lambda i: send(
+                self.own.at[hi], self.own.at[hi], *self.ah, at_h(h_peer(i))
+            ).start())
+
+        def gather_l(self):
+            self.whole[3].wait_recv()
+            every(NL, lambda i: send(self.own, self.own, *self.al, at_l(l_peer(i))).start())
+
         def gather_x(self):
-            self.whole[2].wait_recv()
+            self.whole[4].wait_recv()
             every(nx, lambda i: send(
-                self.full.at[xi], self.full.at[xi], *self.ax_sems, at_x(x_peer(i))
+                self.full.at[xi], self.full.at[xi], *self.ax, at_x(x_peer(i))
             ).start())
 
         def finish(self):
-            self.whole[3].wait_recv()
+            self.whole[5].wait_recv()
 
         def drain(self):
             for copy in self.whole:
                 copy.wait_send()
 
-    dec = Sum(
-        pdec, rxdec, sumdec, rzdec, fulldec,
-        dx_send, dx_recv, dz_send, dz_recv, daz_send, daz_recv, dax_send, dax_recv,
-    )
-    enc = Sum(
-        pq, rxq, sumq, rzq, fullq,
-        qx_send, qx_recv, qz_send, qz_recv, qaz_send, qaz_recv, qax_send, qax_recv,
-    )
+    dec = Sum(pdec, rxdec, sumdec, rldec, midec, rhdec, fulldec, *sum_sems[0:6])
+    enc = Sum(pq, rxq, sumq, rlq, midq, rhq, fullq, *sum_sems[6:12])
+
     for load in loads[5:]:
         load.wait()
     lat_query = lq_ref[...]
@@ -242,7 +270,7 @@
         ref[slot, 2:4, :] = delta_rows
 
     put_stats(sx, xi, fold(top + jnp.log(total)), fold(delta))
-    every(nx, lambda i: send(sx.at[xi], sx.at[xi], sx_send, sx_recv, at_x(x_peer(i))).start())
+    every(nx, lambda i: send(sx.at[xi], sx.at[xi], *sx_sems, at_x(x_peer(i))).start())
 
     key_sum = jnp.zeros((LAT, DH), F32)
     value_sum = jnp.zeros((LAT, DH), F32)
@@ -250,14 +278,14 @@
         valid = mcol[span, :].astype(BF16)
         key_sum = key_sum + dot(dscore[:, span], pq_ref[span, :] * valid, NN)
         value_sum = value_sum + dot(dprob[:, span], dg_ref[span, :] * valid, NN)
-    pdec[0:nx // 2] = key_sum.reshape(nx // 2, NZ, 8, 128)
-    pdec[nx // 2:nx] = value_sum.reshape(nx // 2, NZ, 8, 128)
+    pdec[0:nx // 2] = key_sum.reshape(nx // 2, NL, NH, 8, 128)
+    pdec[nx // 2:nx] = value_sum.reshape(nx // 2, NL, NH, 8, 128)
     dec.scatter_x()
 
-    sx_all = all_of(sx, nx, sx_send, sx_recv, at_x(x_peer(1)))
+    sx_all = all_of(sx, nx, *sx_sems, at_x(x_peer(1)))
     sx_all.wait_recv()
-    put_stats(sz, zi, *merge_stats(sx, nx))
-    every(NZ, lambda i: send(sz.at[zi], sz.at[zi], sz_send, sz_recv, at_z(z_peer(i))).start())
+    put_stats(sl, li, *merge_stats(sx, nx))
+    every(NL, lambda i: send(sl.at[li], sl.at[li], *sl_sems, at_l(l_peer(i))).start())
 
     a = jnp.zeros((DH, LAT), F32)
     b = jnp.zeros((DH, LAT), F32)
@@ -273,31 +301,36 @@
 
     for i in range(nx):
         for j in range(NZ):
-            pq[i, j] = jnp.concatenate([a[place(i, j)], b[place(i, j)]], axis=0)
+            pq[i, j // NH, j % NH] = jnp.concatenate([a[place(i, j)], b[place(i, j)]], axis=0)
     enc.scatter_x()
+
+    sl_all = all_of(sl, NL, *sl_sems, at_l(l_peer(1)))
+    sl_all.wait_recv()
+    put_stats(sh, hi, *merge_stats(sl, NL))
+    every(NH, lambda i: send(sh.at[hi], sh.at[hi], *sh_sems, at_h(h_peer(i))).start())
+
+    dec.gathered_x()
+    sumdec[...] = tree_sum([rxdec[i] for i in range(nx)])
+    dec.scatter_l()
 
     for span in spans:
         grad = dot(dscore[:, span], lat_key, TN) * (mcol[span, :] * scale)
         gpq_ref[span, :] = grad.astype(BF16)
 
-    dec.gathered_x()
-    sumdec[...] = (rxdec[0] + rxdec[1]) + (rxdec[2] + rxdec[3])
-    dec.scatter_z()
-
-    sz_all = all_of(sz, NZ, sz_send, sz_recv, at_z(z_peer(1)))
-    sz_all.wait_recv()
-    lse2, delta2 = merge_stats(sz, NZ)
+    sh_all = all_of(sh, NH, *sh_sems, at_h(h_peer(1)))
+    sh_all.wait_recv()
+    lse2, delta2 = merge_stats(sh, NH)
     enc.gathered_x()
     factors = [jnp.exp(sx[i, 0:2, :] - lse2) for i in range(nx)]
     shifts = [sx[i, 2:4, :] - delta2 for i in range(nx)]
     for j in range(NZ):
         half = slice(j % 2, j % 2 + 1)
         terms = [
-            factors[i][half] * (rxq[i, j, 0:4, :] + shifts[i][half] * rxq[i, j, 4:8, :])
+            factors[i][half] * (rxq[i, j // NH, j % NH, 0:4, :] + shifts[i][half] * rxq[i, j // NH, j % NH, 4:8, :])
             for i in range(nx)
         ]
-        sumq[j] = functools.reduce(jnp.add, terms)
-    enc.scatter_z()
+        sumq[j // NH, j % NH] = functools.reduce(jnp.add, terms)
+    enc.scatter_l()
 
     lse = jnp.concatenate([lse2[0:1], lse2[1:2]], axis=1)
     delta = jnp.concatenate([delta2[0:1], delta2[1:2]], axis=1)
@@ -309,10 +342,16 @@
             gpk_ref[span, :] = (dot(ds, lat_query, NN) * scale).astype(BF16)
             gpv_ref[span, :] = dot(p.astype(BF16), enc_grad, NN).astype(BF16)
 
-    enc_packets(0, 3)
-    dec.gather_z()
-    enc_packets(3, len(spans))
-    enc.gather_z()
+    enc_packets(0, 2)
+    dec.scatter_h()
+    enc_packets(2, 3)
+    enc.scatter_h()
+    enc_packets(3, 4)
+    dec.gather_h()
+    enc.gather_h()
+    enc_packets(4, len(spans))
+    dec.gather_l()
+    enc.gather_l()
     dec.gather_x()
     enc.gather_x()
     dec.finish()
@@ -324,13 +363,14 @@
             for c in range(2):
                 at, lanes = place(i, k + c)
                 query_t[at.start:at.start + 8, lanes] = jnp.concatenate(
-                    [fullq[i, k + c], fullq[i, k + 2 + c]], axis=0
+                    [fullq[i, j // NH, j % NH] for j in (k + c, k + 2 + c)], axis=0
                 )
     glq_ref[...] = (query_t[...].T * scale).astype(BF16)
 
     mask_all.wait_send()
     sx_all.wait_send()
-    sz_all.wait_send()
+    sl_all.wait_send()
+    sh_all.wait_send()
     dec.drain()
     enc.drain()
 
@@ -365,11 +405,13 @@
 
         def reduce_buffers(sent, depth):
             return [
-                pltpu.VMEM((nx, NZ, sent, 128), F32),
-                pltpu.VMEM((nx, NZ, sent, 128), F32),
-                pltpu.VMEM((NZ, depth, 128), F32),
-                pltpu.VMEM((NZ, depth, 128), F32),
-                pltpu.VMEM((nx, NZ, depth, 128), F32),
+                pltpu.VMEM((nx, NL, NH, sent, 128), F32),
+                pltpu.VMEM((nx, NL, NH, sent, 128), F32),
+                pltpu.VMEM((NL, NH, depth, 128), F32),
+                pltpu.VMEM((NL, NH, depth, 128), F32),
+                pltpu.VMEM((NH, depth, 128), F32),
+                pltpu.VMEM((NH, depth, 128), F32),
+                pltpu.VMEM((nx, NL, NH, depth, 128), F32),
             ]
 
         made = pl.pallas_call(
@@ -388,12 +430,13 @@
                 pltpu.VMEM((LAT, rows), BF16),
                 pltpu.VMEM((DH, LAT), F32),
                 pltpu.VMEM((nx, 4, 128), F32),
-                pltpu.VMEM((NZ, 4, 128), F32),
+                pltpu.VMEM((NL, 4, 128), F32),
+                pltpu.VMEM((NH, 4, 128), F32),
             ]
             + reduce_buffers(8, 8)
             + reduce_buffers(8, 4)
             + [pltpu.SemaphoreType.DMA((len(args),))]
-            + [pltpu.SemaphoreType.DMA((1,))] * 22,
+            + [pltpu.SemaphoreType.DMA((1,))] * 32,
             compiler_params=pltpu.CompilerParams(
                 collective_id=0, has_side_effects=True, vmem_limit_bytes=48 * 2**20
             ),

time: 51.5 us -> 60.5 us (1.17)
  the two profiles are of different devices: /device:TPU:32 before, /device:TPU:4 now
where the time goes in v5:
time: 60.5 us; the launch traced here: 60.4 us
  Pallas kernels  59.7 us (99%)
  between operations  0.64 us (1%)
    pallas_call x1, Pallas kernels, on_device(): pl.pallas_call(functools.partial(kernel, nx, nh, rows), out_shape=outs, i...  58.4 us
    pallas_call x1, Pallas kernels, on_device(): pl.pallas_call(write_out, out_shape=outs, in_specs=[vmem] * len(outs), ou...  1.34 us

profile of v5, /device:TPU:4, one launch (start us, length us, event | category | flops | bytes accessed | tf_op | source)
XLA Modules:
  0.0 60.4 jit_solution(10081902739202594270)
XLA Ops:
  0.6 58.4 %perceiver_backward.1 = (bf16[256,128]{1,0:T(8,128)(2,1)S(1)}, bf16[2304,128]{1,0:T(8,128)(2,1)S(1)}, bf16[2304,128]{1,0:T(8,128)(2,1)S(1)}, bf16[2304,128]{1,0:...) custom-call(bf16[256,128]{1,0:T(8,128)(2,1)} %lq_hbm.1, bf16[2304,128]{1,0:T(8,128)(2,1)} %pk_hbm.1, ...), custom_call_target="tpu_custom_call" | custom-call | tf_op jit(solution)/shard_map/perceiver_backward/pallas_call | solution.py:417
  59.0 1.3 %write_out.1 = (bf16[256,128]{1,0:T(8,128)(2,1)}, bf16[2304,128]{1,0:T(8,128)(2,1)}, bf16[2304,128]{1,0:T(8,128)(2,1)}, bf16[2304,128]{1,0:T(8,128)(2,1)}, bf16[256,128]{1,0:T(8,128)(2,1)}, /*index=5*/f32[256,128]{1,0:T(8,128)}) custom-call(bf16[256,128]{1,0:T(8,128)(2,1)S(1)} %get-tuple-element.12.refs_0_, bf16[2304,128]{1,0:T(8,128)(2,1)S(1)} %get-tuple-element.13.refs_1_, ...), custom_call_target="tpu_custom_call" | custom-call | tf_op jit(solution)/shard_map/write_out/pallas_call | solution.py:445

commit v6 on v2

--- a/solution.py
+++ b/solution.py
@@ -10,7 +10,8 @@
 
 DH = 128
 LAT = 256
-NZ = 16
+Z = 16
+NZ = 8
 MESH = pl.DeviceIdType.MESH
 F32 = jnp.float32
 BF16 = jnp.bfloat16
@@ -30,6 +31,12 @@
     total = functools.reduce(jnp.add, weights)
     mixed = functools.reduce(jnp.add, [w * ref[i, 2:4, :] for i, w in enumerate(weights)])
     return top + jnp.log(total), mixed / total
+
+
+def tree_sum(pieces):
+    while len(pieces) > 1:
+        pieces = [a + b for a, b in zip(pieces[0::2], pieces[1::2])]
+    return pieces[0]
 
 
 def fold(line):
@@ -54,8 +61,9 @@
     spans = [slice(at, at + size) for at in range(0, rows, size)]
     seq = lax.axis_index("seq")
     head = lax.axis_index("head")
-    xi = seq // NZ
-    zi = lax.rem(seq, NZ)
+    low = Z // NZ
+    xi = (seq // Z) * low + lax.rem(seq, low)
+    zi = lax.rem(seq, Z) // low
 
     loads = [
         pltpu.make_async_copy(src, dst, in_sems.at[i])
@@ -89,10 +97,10 @@
         return (seq, peer)
 
     def at_x(peer):
-        return (peer * NZ + zi, head)
+        return ((peer // low) * Z + zi * low + lax.rem(peer, low), head)
 
     def at_z(peer):
-        return (xi * NZ + peer, head)
+        return ((xi // low) * Z + peer * low + lax.rem(xi, low), head)
 
     def every(count, body):
         def step(i, carry):
@@ -180,10 +188,7 @@
         def gather_z(self):
             self.rz[zi] = self.summed[zi]
             self.whole[1].wait_recv()
-            pieces = [self.rz[i] for i in range(NZ)]
-            while len(pieces) > 1:
-                pieces = [a + b for a, b in zip(pieces[0::2], pieces[1::2])]
-            self.full[xi, zi] = pieces[0]
+            self.full[xi, zi] = tree_sum([self.rz[i] for i in range(NZ)])
             every(NZ, lambda i: send(
                 self.full.at[xi, zi], self.full.at[xi, zi], *self.az_sems, at_z(z_peer(i))
             ).start())
@@ -244,6 +249,23 @@
     put_stats(sx, xi, fold(top + jnp.log(total)), fold(delta))
     every(nx, lambda i: send(sx.at[xi], sx.at[xi], sx_send, sx_recv, at_x(x_peer(i))).start())
 
+    a = jnp.zeros((DH, LAT), F32)
+    b = jnp.zeros((DH, LAT), F32)
+    for span, w, d in zip(spans, shares, deltas):
+        sums = dot(pk_ref[span, :], esums[span, :], TN)
+        w = w * inverse
+        a = a + w * (sums[:, :LAT] + (d - delta) * sums[:, LAT:])
+        b = b + w * sums[:, LAT:]
+
+    def place(i, j):
+        at = i * (DH // nx) + (j // 2) * 4
+        return slice(at, at + 4), slice((j % 2) * 128, (j % 2) * 128 + 128)
+
+    for i in range(nx):
+        for j in range(NZ):
+            pq[i, j] = jnp.concatenate([a[place(i, j)], b[place(i, j)]], axis=0)
+    enc.scatter_x()
+
     key_sum = jnp.zeros((LAT, DH), F32)
     value_sum = jnp.zeros((LAT, DH), F32)
     for span in spans:
@@ -259,30 +281,9 @@
     put_stats(sz, zi, *merge_stats(sx, nx))
     every(NZ, lambda i: send(sz.at[zi], sz.at[zi], sz_send, sz_recv, at_z(z_peer(i))).start())
 
-    a = jnp.zeros((DH, LAT), F32)
-    b = jnp.zeros((DH, LAT), F32)
-    for span, w, d in zip(spans, shares, deltas):
-        sums = dot(pk_ref[span, :], esums[span, :], TN)
-        w = w * inverse
-        a = a + w * (sums[:, :LAT] + (d - delta) * sums[:, LAT:])
-        b = b + w * sums[:, LAT:]
-
-    def place(i, j):
-        at = i * (DH // nx) + (j // 2) * 4
-        return slice(at, at + 4), slice((j % 2) * 128, (j % 2) * 128 + 128)
-
-    for i in range(nx):
-        for j in range(NZ):
-            pq[i, j] = jnp.concatenate([a[place(i, j)], b[place(i, j)]], axis=0)
-    enc.scatter_x()
-
     for span in spans:
         grad = dot(dscore[:, span], lat_key, TN) * (mcol[span, :] * scale)
         gpq_ref[span, :] = grad.astype(BF16)
-
-    dec.gathered_x()
-    sumdec[...] = (rxdec[0] + rxdec[1]) + (rxdec[2] + rxdec[3])
-    dec.scatter_z()
 
     sz_all = all_of(sz, NZ, sz_send, sz_recv, at_z(z_peer(1)))
     sz_all.wait_recv()
@@ -299,6 +300,10 @@
         sumq[j] = functools.reduce(jnp.add, terms)
     enc.scatter_z()
 
+    dec.gathered_x()
+    sumdec[...] = tree_sum([rxdec[i] for i in range(nx)])
+    dec.scatter_z()
+
     lse = jnp.concatenate([lse2[0:1], lse2[1:2]], axis=1)
     delta = jnp.concatenate([delta2[0:1], delta2[1:2]], axis=1)
 
@@ -310,14 +315,12 @@
             gpv_ref[span, :] = dot(p.astype(BF16), enc_grad, NN).astype(BF16)
 
     enc_packets(0, 3)
+    enc.gather_z()
+    enc_packets(3, 4)
     dec.gather_z()
-    enc_packets(3, len(spans))
-    enc.gather_z()
+    enc_packets(4, len(spans))
+    enc.gather_x()
     dec.gather_x()
-    enc.gather_x()
-    dec.finish()
-    glk_ref[...] = (fulldec[0:nx // 2].reshape(LAT, DH) * scale).astype(BF16)
-    glv_ref[...] = fulldec[nx // 2:nx].reshape(LAT, DH)
     enc.finish()
     for i in range(nx):
         for k in range(0, NZ, 4):
@@ -327,6 +330,10 @@
                     [fullq[i, k + c], fullq[i, k + 2 + c]], axis=0
                 )
     glq_ref[...] = (query_t[...].T * scale).astype(BF16)
+
+    dec.finish()
+    glk_ref[...] = (fulldec[0:nx // 2].reshape(LAT, DH) * scale).astype(BF16)
+    glv_ref[...] = fulldec[nx // 2:nx].reshape(LAT, DH)
 
     mask_all.wait_send()
     sx_all.wait_send()

time: 51.5 us -> 55.2 us (1.072)
  Pallas kernels: 50.7 us -> 54.5 us
    pallas_call x1, Pallas kernels: 49.4 us -> 53.1 us  [on_device(): pl.pallas_call(functools.partial(kernel, nx, nh, rows), out_shape=outs, i...]
where the time goes in v6:
time: 55.2 us; the launch traced here: 55.1 us
  Pallas kernels  54.5 us (99%)
  between operations  0.64 us (1%)
    pallas_call x1, Pallas kernels, on_device(): pl.pallas_call(functools.partial(kernel, nx, nh, rows), out_shape=outs, i...  53.1 us
    pallas_call x1, Pallas kernels, on_device(): pl.pallas_call(write_out, out_shape=outs, in_specs=[vmem] * len(outs), ou...  1.34 us

profile of v6, /device:TPU:32, one launch (start us, length us, event | category | flops | bytes accessed | tf_op | source)
XLA Modules:
  0.0 55.1 jit_solution(3658440225155304154)
XLA Ops:
  0.6 53.1 %perceiver_backward.1 = (bf16[256,128]{1,0:T(8,128)(2,1)S(1)}, bf16[2304,128]{1,0:T(8,128)(2,1)S(1)}, bf16[2304,128]{1,0:T(8,128)(2,1)S(1)}, bf16[2304,128]{1,0:...) custom-call(bf16[256,128]{1,0:T(8,128)(2,1)} %lq_hbm.1, bf16[2304,128]{1,0:T(8,128)(2,1)} %pk_hbm.1, ...), custom_call_target="tpu_custom_call" | custom-call | tf_op jit(solution)/shard_map/perceiver_backward/pallas_call | solution.py:382
  53.8 1.3 %write_out.1 = (bf16[256,128]{1,0:T(8,128)(2,1)}, bf16[2304,128]{1,0:T(8,128)(2,1)}, bf16[2304,128]{1,0:T(8,128)(2,1)}, bf16[2304,128]{1,0:T(8,128)(2,1)}, bf16[256,128]{1,0:T(8,128)(2,1)}, /*index=5*/f32[256,128]{1,0:T(8,128)}) custom-call(bf16[256,128]{1,0:T(8,128)(2,1)S(1)} %get-tuple-element.12.refs_0_, bf16[2304,128]{1,0:T(8,128)(2,1)S(1)} %get-tuple-element.13.refs_1_, ...), custom_call_target="tpu_custom_call" | custom-call | tf_op jit(solution)/shard_map/write_out/pallas_call | solution.py:409

commit v7 on v2

--- a/solution.py
+++ b/solution.py
@@ -145,6 +145,12 @@
         dprob[:, span] = p.astype(BF16)
         dscore[:, span] = (p * (dg - dd)).astype(BF16)
 
+    for load in loads[5:]:
+        load.wait()
+    enc_grad = eg_ref[...]
+    for span in spans:
+        edot[span, :] = dot(pv_ref[span, :], enc_grad, NT)
+
     mask_all = all_of(maskbuf, nh, m_send, m_recv, at_head(head_peer(1)))
     mask_all.wait_recv()
     for h in range(nh):
@@ -209,20 +215,16 @@
         pq, rxq, sumq, rzq, fullq,
         qx_send, qx_recv, qz_send, qz_recv, qaz_send, qaz_recv, qax_send, qax_recv,
     )
-    for load in loads[5:]:
-        load.wait()
     lat_query = lq_ref[...]
-    enc_grad = eg_ref[...]
     tops, totals, deltas = [], [], []
     for span in spans:
         bias = (mcol[span, :] - 1.0) * 1e30
         score = dot(pk_ref[span, :], lat_query, NT) * scale
         score = score + jnp.concatenate([bias, bias], axis=1)
-        grad = dot(pv_ref[span, :], enc_grad, NT)
+        grad = edot[span, :]
         own = jnp.max(score, axis=0, keepdims=True)
         e = jnp.exp(score - own)
         expo[span, :] = e
-        edot[span, :] = grad
         own_total = jnp.sum(e, axis=0, keepdims=True)
         own_delta = jnp.sum(e * grad, axis=0, keepdims=True) / own_total
         esums[span, :LAT] = (e * (grad - own_delta)).astype(BF16)
@@ -244,6 +246,23 @@
     put_stats(sx, xi, fold(top + jnp.log(total)), fold(delta))
     every(nx, lambda i: send(sx.at[xi], sx.at[xi], sx_send, sx_recv, at_x(x_peer(i))).start())
 
+    a = jnp.zeros((DH, LAT), F32)
+    b = jnp.zeros((DH, LAT), F32)
+    for span, w, d in zip(spans, shares, deltas):
+        sums = dot(pk_ref[span, :], esums[span, :], TN)
+        w = w * inverse
+        a = a + w * (sums[:, :LAT] + (d - delta) * sums[:, LAT:])
+        b = b + w * sums[:, LAT:]
+
+    def place(i, j):
+        at = i * (DH // nx) + (j // 2) * 4
+        return slice(at, at + 4), slice((j % 2) * 128, (j % 2) * 128 + 128)
+
+    for i in range(nx):
+        for j in range(NZ):
+            pq[i, j] = jnp.concatenate([a[place(i, j)], b[place(i, j)]], axis=0)
+    enc.scatter_x()
+
     key_sum = jnp.zeros((LAT, DH), F32)
     value_sum = jnp.zeros((LAT, DH), F32)
     for span in spans:
@@ -258,23 +277,6 @@
     sx_all.wait_recv()
     put_stats(sz, zi, *merge_stats(sx, nx))
     every(NZ, lambda i: send(sz.at[zi], sz.at[zi], sz_send, sz_recv, at_z(z_peer(i))).start())
-
-    a = jnp.zeros((DH, LAT), F32)
-    b = jnp.zeros((DH, LAT), F32)
-    for span, w, d in zip(spans, shares, deltas):
-        sums = dot(pk_ref[span, :], esums[span, :], TN)
-        w = w * inverse
-        a = a + w * (sums[:, :LAT] + (d - delta) * sums[:, LAT:])
-        b = b + w * sums[:, LAT:]
-
-    def place(i, j):
-        at = i * (DH // nx) + (j // 2) * 4
-        return slice(at, at + 4), slice((j % 2) * 128, (j % 2) * 128 + 128)
-
-    for i in range(nx):
-        for j in range(NZ):
-            pq[i, j] = jnp.concatenate([a[place(i, j)], b[place(i, j)]], axis=0)
-    enc.scatter_x()
 
     for span in spans:
         grad = dot(dscore[:, span], lat_key, TN) * (mcol[span, :] * scale)

time: 51.5 us -> 53.1 us (1.031)
  the two profiles are of different devices: /device:TPU:32 before, /device:TPU:4 now
where the time goes in v7:
time: 53.1 us; the launch traced here: 52.9 us
  Pallas kernels  52.3 us (98%)
  between operations  0.64 us (1%)
    pallas_call x1, Pallas kernels, on_device(): pl.pallas_call(functools.partial(kernel, nx, nh, rows), out_shape=outs, i...  50.9 us
    pallas_call x1, Pallas kernels, on_device(): pl.pallas_call(write_out, out_shape=outs, in_specs=[vmem] * len(outs), ou...  1.34 us

profile of v7, /device:TPU:4, one launch (start us, length us, event | category | flops | bytes accessed | tf_op | source)
XLA Modules:
  0.0 52.9 jit_solution(12325978980529649637)
XLA Ops:
  0.6 50.9 %perceiver_backward.1 = (bf16[256,128]{1,0:T(8,128)(2,1)S(1)}, bf16[2304,128]{1,0:T(8,128)(2,1)S(1)}, bf16[2304,128]{1,0:T(8,128)(2,1)S(1)}, bf16[2304,128]{1,0:...) custom-call(bf16[256,128]{1,0:T(8,128)(2,1)} %lq_hbm.1, bf16[2304,128]{1,0:T(8,128)(2,1)} %pk_hbm.1, ...), custom_call_target="tpu_custom_call" | custom-call | tf_op jit(solution)/shard_map/perceiver_backward/pallas_call | solution.py:377
  51.6 1.3 %write_out.1 = (bf16[256,128]{1,0:T(8,128)(2,1)}, bf16[2304,128]{1,0:T(8,128)(2,1)}, bf16[2304,128]{1,0:T(8,128)(2,1)}, bf16[2304,128]{1,0:T(8,128)(2,1)}, bf16[256,128]{1,0:T(8,128)(2,1)}, /*index=5*/f32[256,128]{1,0:T(8,128)}) custom-call(bf16[256,128]{1,0:T(8,128)(2,1)S(1)} %get-tuple-element.12.refs_0_, bf16[2304,128]{1,0:T(8,128)(2,1)S(1)} %get-tuple-element.13.refs_1_, ...), custom_call_target="tpu_custom_call" | custom-call | tf_op jit(solution)/shard_map/write_out/pallas_call | solution.py:404

commit v8 on v2

--- a/solution.py
+++ b/solution.py
@@ -99,7 +99,7 @@
             body(i)
             return carry
 
-        lax.fori_loop(1, count, step, 0)
+        lax.fori_loop(1, count, step, 0, unroll=True)
 
     def send(src, dst, send_sem, recv_sem, target):
         return pltpu.make_async_remote_copy(

time: 51.5 us -> 51.2 us (level)
  no operation moved by 1% of the time
where the time goes in v8:
time: 51.2 us; the launch traced here: 51 us
  Pallas kernels  50.4 us (98%)
  between operations  0.64 us (1%)
    pallas_call x1, Pallas kernels, on_device(): pl.pallas_call(functools.partial(kernel, nx, nh, rows), out_shape=outs, i...  49 us
    pallas_call x1, Pallas kernels, on_device(): pl.pallas_call(write_out, out_shape=outs, in_specs=[vmem] * len(outs), ou...  1.34 us

profile of v8, /device:TPU:32, one launch (start us, length us, event | category | flops | bytes accessed | tf_op | source)
XLA Modules:
  0.0 51.0 jit_solution(7411504640678926381)
XLA Ops:
  0.6 49.0 %perceiver_backward.1 = (bf16[256,128]{1,0:T(8,128)(2,1)S(1)}, bf16[2304,128]{1,0:T(8,128)(2,1)S(1)}, bf16[2304,128]{1,0:T(8,128)(2,1)S(1)}, bf16[2304,128]{1,0:...) custom-call(bf16[256,128]{1,0:T(8,128)(2,1)} %lq_hbm.1, bf16[2304,128]{1,0:T(8,128)(2,1)} %pk_hbm.1, ...), custom_call_target="tpu_custom_call" | custom-call | tf_op jit(solution)/shard_map/perceiver_backward/pallas_call | solution.py:375
  49.7 1.3 %write_out.1 = (bf16[256,128]{1,0:T(8,128)(2,1)}, bf16[2304,128]{1,0:T(8,128)(2,1)}, bf16[2304,128]{1,0:T(8,128)(2,1)}, bf16[2304,128]{1,0:T(8,128)(2,1)}, bf16[256,128]{1,0:T(8,128)(2,1)}, /*index=5*/f32[256,128]{1,0:T(8,128)}) custom-call(bf16[256,128]{1,0:T(8,128)(2,1)S(1)} %get-tuple-element.12.refs_0_, bf16[2304,128]{1,0:T(8,128)(2,1)S(1)} %get-tuple-element.13.refs_1_, ...), custom_call_target="tpu_custom_call" | custom-call | tf_op jit(solution)/shard_map/write_out/pallas_call | solution.py:402
